TPU v7x, 128 devices: a whole 4x4x4 slice. The times are simulated.
128 devices in a mesh: pix: 32 (over x, z, core), lay: 4 (over y).
Axes of the slice: x: 4, y: 4, z: 4, core: 2. Of those that a mesh axis runs over, the one named last changes fastest.
Arguments:
- pixel_stack: float32 [524288, 512], P('pix', 'lay'), may hold values from -4000 to 4000, as said below
Outputs:
- scores: float32 [524288, 512], P(('pix', 'lay'))
- log_scale: float32 [512], P('lay')
Inputs may be any that keep to these rules, and one draw needn't show every extreme that they name: pixel_stack is finite.
All inputs are finite; a program needn't handle non-finite values.
Results may differ from a plain program's by a relative error of at most 0.00013.
Values sent between devices are 32-bit elements; how exact they have to be, the bound alone decides.
No kernel may reach another device: no remote copies, remote signals or barrier semaphores. Data moves between devices by JAX's collectives and lax.ppermute only.
A program may use at most 128 MiB of HBM per device.

v0:
```python
import math

import jax
import jax.numpy as jnp
from jax import lax
from jax.sharding import PartitionSpec as P


def swapped(value, axis, distance):
    mask = 2**distance
    pairs = [(source, source ^ mask) for source in range(lax.axis_size(axis))]
    return lax.ppermute(value, axis, pairs)


def body(pixel_stack):
    regrouped = lax.all_to_all(pixel_stack, "lay", split_axis=0, concat_axis=1, tiled=True)
    total = regrouped.shape[0] * lax.axis_size("pix") * lax.axis_size("lay")
    mean = lax.psum(jnp.sum(regrouped, axis=0), ("pix", "lay")) / total
    centered = regrouped - mean
    spread = lax.psum(jnp.sum(centered * centered, axis=0), ("pix", "lay")) / total
    standard = centered * lax.rsqrt(spread + 1e-05)
    share = spread.shape[0] // lax.axis_size("lay")
    own_spread = lax.dynamic_slice_in_dim(spread, lax.axis_index("lay") * share, share, 0)
    log_scale = 0.5 * jnp.log(own_spread + 1e-05)
    gram = jnp.dot(
        standard.T, standard, precision=lax.Precision.HIGHEST, preferred_element_type=jnp.float32
    )
    levels = lax.axis_size(("pix", "lay")).bit_length() - 1
    for level in range(levels):
        gram = gram + swapped(gram, ("pix", "lay"), level)
    width = gram.shape[0]
    lower = jnp.linalg.cholesky(gram)
    inverse = lax.linalg.triangular_solve(
        lower, jnp.eye(width, dtype=gram.dtype), left_side=True, lower=True
    )
    scores = jnp.dot(
        standard, inverse.T, precision=lax.Precision.HIGHEST, preferred_element_type=jnp.float32
    )
    return (scores * math.sqrt(total), log_scale)


def solution(mesh):
    return jax.shard_map(
        body,
        mesh=mesh,
        in_specs=(P("pix", "lay"),),
        out_specs=(P(("pix", "lay"), None), P("lay")),
        check_vma=False,
    )
```

profile of v0, /device:TPU:0, one launch (start us, length us, event | category | flops | bytes accessed | tf_op | source)
XLA Modules:
  0.0 594.3 jit_solution(16632517005085069601)
XLA Ops:
  0.6 98.3 %all_to_all.19 = f32[4,4096,128]{2,1,0:T(8,128)S(1)} all-to-all(f32[4,4096,128]{2,1,0:T(8,128)} %bitcast.69), channel_id=1, replica_groups=mesh['pix'=32,'lay'=4] {'lay'}, dimensions={0} | all-to-all | bytes 16777216 | tf_op jit(solution)/shard_map/all_to_all | solution.py:16
  102.9 66.0 %psum.14 = f32[512]{0:T(512)S(1)} all-reduce(f32[512]{0:T(512)S(1)} %bitcast.70), channel_id=1, replica_groups=mesh['pix'=32,'lay'=4] {'pix','lay'}, use_global_device_ids=true, to_apply=%region_1.0 | all-reduce | flops 512 | bytes 4096 | tf_op jit(solution)/shard_map/psum | solution.py:18
  173.1 62.7 %psum.15 = f32[512]{0:T(512)S(1)} all-reduce(f32[512]{0:T(512)S(1)} %bitcast.71), channel_id=1, replica_groups=mesh['pix'=32,'lay'=4] {'pix','lay'}, use_global_device_ids=true, to_apply=%region_3.0 | all-reduce | flops 512 | bytes 4096 | tf_op jit(solution)/shard_map/psum | solution.py:20
  235.8 7.3 %subtract_multiply_fusion = f32[4096,4,128]{2,0,1:T(8,128)} fusion(f32[4,128]{1,0:T(4,128)S(1)} %get-tuple-element.31, f32[4,128]{1,0:T(4,128)S(1)} %get-tuple-element.34, f32[4,4096,128]{2,1,0:T(8,128)} %copy-done), kind=kLoop, calls=%fused_computation.5 | loop fusion | flops 4194304 | bytes 16781312 | tf_op jit(solution)/shard_map/mul | solution.py:21
  243.0 9.0 %copy.10 = f32[4096,4,128]{0,2,1:T(8,128)} copy(f32[4096,4,128]{2,0,1:T(8,128)} %subtract_multiply_fusion) | data formatting | bytes 16777216 | tf_op jit(solution)/shard_map/mul | solution.py:21
  252.0 16.4 %fusion.48 = f32[512,512]{0,1:T(8,128)S(1)} fusion(f32[4096,512]{0,1:T(8,128)} %bitcast.68), kind=kOutput, calls=%fused_computation.91 | convolution fusion | flops 12884901888 | bytes 9437184 | tf_op jit(solution)/shard_map/dot_general | solution.py:25
  269.3 24.1 %collective-permute-done = f32[512,512]{0,1:T(8,128)S(1)} collective-permute-done((f32[512,512]{0,1:T(8,128)S(1)}, f32[512,512]{0,1:T(8,128)S(1)}, u32[]{:S(2)}, u32[]{:S(2)}) %collective-permute-start) | collective-permute-done | bytes 1048608 | tf_op jit(solution)/shard_map/ppermute | solution.py:12
  295.3 23.9 %collective-permute-done.1 = f32[512,512]{0,1:T(8,128)S(1)} collective-permute-done((f32[512,512]{0,1:T(8,128)S(1)}, f32[512,512]{0,1:T(8,128)S(1)}, u32[]{:S(2)}, u32[]{:S(2)}) %collective-permute-start.1) | collective-permute-done | bytes 1048608 | tf_op jit(solution)/shard_map/ppermute | solution.py:12
  323.0 24.7 %collective-permute-done.3 = f32[512,512]{0,1:T(8,128)S(1)} collective-permute-done((f32[512,512]{0,1:T(8,128)S(1)}, f32[512,512]{0,1:T(8,128)S(1)}, u32[]{:S(2)}, u32[]{:S(2)}) %collective-permute-start.3) | collective-permute-done | bytes 1048608 | tf_op jit(solution)/shard_map/ppermute | solution.py:12
  349.4 24.5 %collective-permute-done.4 = f32[512,512]{0,1:T(8,128)S(1)} collective-permute-done((f32[512,512]{0,1:T(8,128)S(1)}, f32[512,512]{0,1:T(8,128)S(1)}, u32[]{:S(2)}, u32[]{:S(2)}) %collective-permute-start.4) | collective-permute-done | bytes 1048608 | tf_op jit(solution)/shard_map/ppermute | solution.py:12
  374.8 9.0 %copy.9 = f32[4096,4,128]{0,2,1:T(8,128)} copy(f32[4096,4,128]{2,0,1:T(8,128)} %bitcast.67) | data formatting | bytes 16777216 | tf_op jit(solution)/shard_map/all_to_all | solution.py:16
  384.4 13.2 %collective-permute-done.5 = f32[512,512]{0,1:T(8,128)S(1)} collective-permute-done((f32[512,512]{0,1:T(8,128)S(1)}, f32[512,512]{0,1:T(8,128)S(1)}, u32[]{:S(2)}, u32[]{:S(2)}) %collective-permute-start.5) | collective-permute-done | bytes 1048608 | tf_op jit(solution)/shard_map/ppermute | solution.py:12
  399.6 8.4 %fusion = f32[4096,512]{0,1:T(8,128)} fusion(f32[4096,4,128]{0,2,1:T(8,128)} %copy.9, f32[512]{0:T(512)S(1)} %get-tuple-element.32, f32[512]{0:T(512)S(1)} %get-tuple-element.33), kind=kLoop, calls=%fused_computation.3 | loop fusion | flops 4194304 | bytes 16781312 | tf_op jit(solution)/shard_map/mul | solution.py:21
  408.0 14.3 %collective-permute-done.6 = f32[512,512]{0,1:T(8,128)S(1)} collective-permute-done((f32[512,512]{0,1:T(8,128)S(1)}, f32[512,512]{0,1:T(8,128)S(1)}, u32[]{:S(2)}, u32[]{:S(2)}) %collective-permute-start.6) | collective-permute-done | bytes 1048608 | tf_op jit(solution)/shard_map/ppermute | solution.py:12
  424.0 11.7 %cholesky.104 = f32[128,128]{1,0:T(8,128)S(1)} custom-call(f32[128,128]{1,0:T(8,128)S(1)} %cholesky.266), custom_call_target="Cholesky" | custom-call | tf_op jit(solution)/shard_map/jit(cholesky)/cholesky | solution.py:32
  435.9 9.8 %custom-call.30 = f32[1,128,128]{1,2,0:T(8,128)S(1)} custom-call(f32[1,128,128]{2,1,0:T(8,128)S(1)} %get-tuple-element.29), custom_call_target="InvertDiagBlocksLowerTriangular" | custom-call | tf_op jit(solution)/shard_map/jit(cholesky)/cholesky | solution.py:32
  448.2 11.8 %cholesky.217 = f32[128,128]{1,0:T(8,128)S(1)} custom-call(f32[128,128]{1,0:T(8,128)S(1)} %cholesky.270), custom_call_target="Cholesky" | custom-call | tf_op jit(solution)/shard_map/jit(cholesky)/cholesky | solution.py:32
  460.1 9.8 %custom-call.31 = f32[1,128,128]{1,2,0:T(8,128)S(1)} custom-call(f32[1,128,128]{2,1,0:T(8,128)S(1)} %get-tuple-element.26), custom_call_target="InvertDiagBlocksLowerTriangular" | custom-call | tf_op jit(solution)/shard_map/jit(cholesky)/cholesky | solution.py:32
  471.5 11.7 %cholesky.238 = f32[128,128]{1,0:T(8,128)S(1)} custom-call(f32[128,128]{1,0:T(8,128)S(1)} %cholesky.275), custom_call_target="Cholesky" | custom-call | tf_op jit(solution)/shard_map/jit(cholesky)/cholesky | solution.py:32
  483.9 9.8 %custom-call.32 = f32[1,128,128]{1,2,0:T(8,128)S(1)} custom-call(f32[1,128,128]{2,1,0:T(8,128)S(1)} %get-tuple-element.23), custom_call_target="InvertDiagBlocksLowerTriangular" | custom-call | tf_op jit(solution)/shard_map/jit(cholesky)/cholesky | solution.py:32
  495.1 11.9 %cholesky.255 = f32[128,128]{1,0:T(8,128)S(1)} custom-call(f32[128,128]{1,0:T(8,128)S(1)} %slice_subtract_fusion.2), custom_call_target="Cholesky" | custom-call | tf_op jit(solution)/shard_map/jit(cholesky)/cholesky | solution.py:32
  510.9 10.1 %while.1 = (s32[]{:T(128)}, f32[512,512]{1,0:T(8,128)S(1)}, s32[4,2]{0,1:T(2,128)S(1)}, f32[4,128,128]{2,1,0:T(8,128)}, s32[]{:T(128)}) while((s32[]{:T(128)}, f32[512,512]{1,0:T(8,128)S(1)}, s32[4,2]{0,1:T(2,128)S(1)}, f32[4,128,128]{2,1,0:T(8,128)}, s32[]{:T(128)}) %tuple.34), condition=%wide.while_cond, body=%wide.while_body.sunk | while | flops 2 | bytes 132705 | solution.py:33
  521.0 40.1 %custom-call.33 = f32[4,128,128]{1,2,0:T(8,128)S(1)} custom-call(f32[4,128,128]{2,1,0:T(8,128)} %get-tuple-element.9), custom_call_target="InvertDiagBlocksLowerTriangular" | custom-call | tf_op jit(solution)/shard_map/triangular_solve | solution.py:33
  564.2 29.7 %convolution_multiply_fusion = f32[4096,512]{1,0:T(8,128)} fusion(f32[4096,512]{0,1:T(8,128)} %fusion, f32[128,512]{1,0:T(8,128)S(1)} %fusion.30, f32[128,512]{1,0:T(8,128)S(1)} %fusion.31, f32[128,512]{1,0:T(8,128)S(1)} %fusion.33, f32[128,512]{1,0:T(8,128)S(1)} %fusion.20), kind=kOutput, calls=%fused_computation.6 | convolution fusion | flops 12887785472 | bytes 17825792 | tf_op jit(solution)/shard_map/dot_general | solution.py:36
  (68 shorter events, 42.6 us)
Async XLA Ops:
  98.9 3.4 copy-start
  268.4 25.0 %collective-permute-start = (f32[512,512]{0,1:T(8,128)S(1)}, f32[512,512]{0,1:T(8,128)S(1)}, u32[]{:S(2)}, u32[]{:S(2)}) collective-permute-start(f32[512,512]{0,1:T(8,128)S(1)} %fusion.48), channel_id=1, source_target_pairs={{0,1},{1,0},{2,3},{3,2},{4,5},{5,4},{6,7},{7,6},{8,9},{9,8},{10,11... | collective-permute-start | bytes 3145736 | tf_op jit(solution)/shard_map/ppermute | solution.py:12
  293.6 25.6 %collective-permute-start.1 = (f32[512,512]{0,1:T(8,128)S(1)}, f32[512,512]{0,1:T(8,128)S(1)}, u32[]{:S(2)}, u32[]{:S(2)}) collective-permute-start(f32[512,512]{0,1:T(8,128)S(1)} %add.82), channel_id=1, source_target_pairs={{0,2},{1,3},{2,0},{3,1},{4,6},{5,7},{6,4},{7,5},{8,10},{9,11},{10,... | collective-permute-start | bytes 3145736 | tf_op jit(solution)/shard_map/ppermute | solution.py:12
  319.4 2.7 collective-permute-start.2
  322.4 25.3 %collective-permute-start.3 = (f32[512,512]{0,1:T(8,128)S(1)}, f32[512,512]{0,1:T(8,128)S(1)}, u32[]{:S(2)}, u32[]{:S(2)}) collective-permute-start(f32[512,512]{0,1:T(8,128)S(1)} %add.84), channel_id=1, source_target_pairs={{0,8},{1,9},{2,10},{3,11},{4,12},{5,13},{6,14},{7,15},{8,0},{9,1},... | collective-permute-start | bytes 3145736 | tf_op jit(solution)/shard_map/ppermute | solution.py:12
  347.9 26.0 %collective-permute-start.4 = (f32[512,512]{0,1:T(8,128)S(1)}, f32[512,512]{0,1:T(8,128)S(1)}, u32[]{:S(2)}, u32[]{:S(2)}) collective-permute-start(f32[512,512]{0,1:T(8,128)S(1)} %add.85), channel_id=1, source_target_pairs={{0,16},{1,17},{2,18},{3,19},{4,20},{5,21},{6,22},{7,23},{8,24},{9,... | collective-permute-start | bytes 3145736 | tf_op jit(solution)/shard_map/ppermute | solution.py:12
  374.1 23.5 %collective-permute-start.5 = (f32[512,512]{0,1:T(8,128)S(1)}, f32[512,512]{0,1:T(8,128)S(1)}, u32[]{:S(2)}, u32[]{:S(2)}) collective-permute-start(f32[512,512]{0,1:T(8,128)S(1)} %add.86), channel_id=1, source_target_pairs={{0,32},{1,33},{2,34},{3,35},{4,36},{5,37},{6,38},{7,39},{8,40},{9,... | collective-permute-start | bytes 3145736 | tf_op jit(solution)/shard_map/ppermute | solution.py:12
  397.8 24.5 %collective-permute-start.6 = (f32[512,512]{0,1:T(8,128)S(1)}, f32[512,512]{0,1:T(8,128)S(1)}, u32[]{:S(2)}, u32[]{:S(2)}) collective-permute-start(f32[512,512]{0,1:T(8,128)S(1)} %add.87), channel_id=1, source_target_pairs={{0,64},{1,65},{2,66},{3,67},{4,68},{5,69},{6,70},{7,71},{8,72},{9,... | collective-permute-start | bytes 3145736 | tf_op jit(solution)/shard_map/ppermute | solution.py:12
  423.0 1.0 copy-start.1
where the time goes:
time: 604 us; the launch traced here: 594 us
  blocking collectives  227 us (38%)
  other arithmetic  142 us (24%)
  waiting for transfers between devices  127 us (21%)
  matrix products  54.5 us (9%)
  local copies, waits for them, and re-layouts  32.8 us (5%)
  starting transfers between devices  7.14 us (1%)
    ppermute x7, waiting for transfers between devices, swapped(): return lax.ppermute(value, axis, pairs)  127 us
    all_to_all x1, blocking collectives, body(): lax.all_to_all(pixel_stack, 'lay', split_axis=0, concat_axis=1, tiled=True)  98.3 us
    another operation x14, other arithmetic, body(): lower = jnp.linalg.cholesky(gram)  78.7 us
    psum x1, blocking collectives, body(): mean = lax.psum(jnp.sum(regrouped, axis=0), ('pix', 'lay')) / total  66 us
    psum x1, blocking collectives, body(): lax.psum(jnp.sum(centered * centered, axis=0), ('pix', 'lay')) / total  62.7 us
    another operation x3, other arithmetic, body(): lax.linalg.triangular_solve(lower, jnp.eye(width, dtype=gram.dtype), left...  40.2 us
    dot_general x1, matrix products, body(): jnp.dot(standard, inverse.T, precision=lax.Precision.HIGHEST, preferred_e...  29.7 us
    dot_general x1, matrix products, body(): jnp.dot(standard.T, standard, precision=lax.Precision.HIGHEST, preferred_...  16.4 us
  transfers between devices with their start and end apart: 7, of which 7 were waited for; matrix products, arithmetic and copies ran while one was open for 3% of the time, Pallas kernels for 0%

commit v1 on v0

v1 whole, which is shorter than its diff:
```python
import functools

import jax
import jax.numpy as jnp
from jax import lax
from jax.experimental import pallas as pl
from jax.experimental.pallas import tpu as pltpu
from jax.sharding import Mesh
from jax.sharding import PartitionSpec as P

EXACT = lax.Precision.HIGHEST
LANES = 128
CHUNKS = 2
TILE = 512
VMEM_LIMIT = 48 * 2**20


def dot(a, b, contract, precision=None):
    return lax.dot_general(
        a, b, (contract, ((), ())), precision=precision, preferred_element_type=jnp.float32
    )


def gram_kernel(last, first, place, own, near, far, back, mean, *rest):
    rest = list(rest)
    held = None if first else rest.pop(0)
    if not first:
        rest.pop(0), rest.pop(0)
    high, low, sums = rest[:3]
    packed = rest[3] if last else None
    step = pl.program_id(0)

    @pl.when(step == 0)
    def _():
        sums[...] = jnp.zeros_like(sums) if first else held[...]

    for away, ref in enumerate((own, near, far, back)):
        layer = lax.rem(place[0] - away + 4, 4)
        lanes = pl.ds(pl.multiple_of(layer * LANES, LANES), LANES)
        value = ref[...].reshape(-1, LANES) - mean[0:1, lanes]
        top = value.astype(jnp.bfloat16)
        high[:, lanes] = top
        low[:, lanes] = (value - top.astype(jnp.float32)).astype(jnp.bfloat16)

    rows = ((0,), (0,))
    half = 2 * LANES
    a, b = high[:, :half], high[:, half:]
    al, bl = low[:, :half], low[:, half:]
    sums[0] += dot(a, a, rows)
    sums[1] += dot(b, b, rows)
    sums[2] += dot(b, a, rows) + dot(b, al, rows) + dot(bl, a, rows)
    sums[3] += dot(a, al, rows)
    sums[4] += dot(b, bl, rows)

    if last:

        @pl.when(step == pl.num_programs(0) - 1)
        def _():
            for side in range(2):
                cross = sums[3 + side]
                whole = sums[side] + cross + cross.T
                packed[5 * side] = whole[:LANES, :LANES]
                packed[5 * side + 1] = whole[LANES:, :LANES]
                packed[5 * side + 2] = whole[LANES:, LANES:]
            packed[3] = sums[2, :LANES, :LANES]
            packed[4] = sums[2, LANES:, :LANES]
            packed[8] = sums[2, :LANES, LANES:]
            packed[9] = sums[2, LANES:, LANES:]


BLOCKS = ((0, 0), (1, 0), (1, 1), (2, 0), (3, 0), (2, 2), (3, 2), (3, 3), (2, 1), (3, 1))


def gram_chunk(chunk, place, blocks, pieces, mean, carried):
    rows = pieces[0].shape[0]
    steps = rows // TILE
    pixels, width = blocks.shape[1], 4 * LANES
    first, last = chunk == 0, chunk == CHUNKS - 1
    at = chunk * steps
    piece = pl.BlockSpec((TILE, LANES), lambda t, y: (t, 0))
    whole = pl.BlockSpec((5, 256, 256), lambda t, y: (0, 0, 0))
    half = pl.BlockSpec((TILE, width), lambda t, y: (t + at, 0))
    in_specs = [
        pl.BlockSpec((1, TILE, LANES), lambda t, y: (y[0], t + at, 0)),
        piece,
        piece,
        piece,
        pl.BlockSpec((1, width), lambda t, y: (0, 0)),
    ]
    args = [place, blocks, *pieces, mean]
    aliases = {}
    if not first:
        high, low, sums = carried
        in_specs += [whole, pl.BlockSpec(memory_space=pl.ANY), pl.BlockSpec(memory_space=pl.ANY)]
        args += [sums, high, low]
        aliases = {6: 2, 7: 0, 8: 1}
    out_specs = [half, half, whole]
    out_shape = [
        jax.ShapeDtypeStruct((pixels, width), jnp.bfloat16),
        jax.ShapeDtypeStruct((pixels, width), jnp.bfloat16),
        jax.ShapeDtypeStruct((5, 256, 256), jnp.float32),
    ]
    if last:
        out_specs.append(pl.BlockSpec((10, LANES, LANES), lambda t, y: (0, 0, 0)))
        out_shape.append(jax.ShapeDtypeStruct((10, LANES, LANES), jnp.float32))
    return pl.pallas_call(
        functools.partial(gram_kernel, last, first),
        grid_spec=pltpu.PrefetchScalarGridSpec(
            num_scalar_prefetch=1, grid=(steps,), in_specs=in_specs, out_specs=out_specs
        ),
        out_shape=out_shape,
        input_output_aliases=aliases,
        compiler_params=pltpu.CompilerParams(vmem_limit_bytes=VMEM_LIMIT),
        cost_estimate=pl.CostEstimate(
            flops=7 * 2 * rows * 256 * 256, bytes_accessed=rows * width * 8, transcendentals=0
        ),
        name="gram",
    )(*args)


def factor_block(rest, carried):
    outs = []
    row = lax.broadcasted_iota(jnp.int32, (8, LANES), 0)
    for at in range(0, LANES, 8):
        rows = LANES - at
        columns = [jnp.broadcast_to(rest[:, at + c : at + c + 1], (rows, LANES)) for c in range(8)]
        scale = jnp.zeros((8, LANES), jnp.float32)
        for j in range(8):
            pivot = columns[j][j : j + 1, :]
            scale = jnp.where(row == j, lax.rsqrt(jnp.broadcast_to(pivot, (8, LANES))), scale)
            weight = columns[j] * (1.0 / pivot)
            inside = jnp.where(row > j, weight[:8], 0.0)
            weight = jnp.concatenate([inside, weight[8:]], axis=0) if rows > 8 else inside
            for c in range(j + 1, 8):
                columns[c] = columns[c] - weight * columns[c][j : j + 1, :]
            rest = rest - weight * rest[j : j + 1, :]
            carried = carried - weight * carried[j : j + 1, :]
        outs.append(carried[:8] * scale)
        rest, carried = rest[8:], carried[8:]
    return jnp.concatenate(outs, axis=0)


def factor_kernel(pixels, packed, high, low, spread, gram, inverse):
    n = gram.shape[0]
    shape = (LANES, LANES)
    eye = lax.broadcasted_iota(jnp.int32, shape, 0) == lax.broadcasted_iota(jnp.int32, shape, 1)
    across, down = [], []
    for k in range(4):
        index = BLOCKS.index((k, k))
        diagonal = jnp.where(eye, packed[index], 0.0) * (1.0 / pixels)
        flat = jnp.sum(diagonal, axis=0, keepdims=True)
        spread[0:1, k * LANES : (k + 1) * LANES] = flat
        across.append(lax.rsqrt(flat + 1e-05))
        down.append(lax.rsqrt(jnp.sum(diagonal, axis=1, keepdims=True) + 1e-05))
    for index, (i, j) in enumerate(BLOCKS):
        block = packed[index] * (1.0 / pixels) * down[i] * across[j]
        gram[i * LANES : (i + 1) * LANES, j * LANES : (j + 1) * LANES] = block
        if i != j:
            gram[j * LANES : (j + 1) * LANES, i * LANES : (i + 1) * LANES] = block.T
    plain = ((1,), (0,))
    for at in range(0, n, LANES):
        end = at + LANES
        here = slice(at, end)
        own = factor_block(gram[here, here], jnp.where(eye, 1.0, 0.0))
        if at > 0:
            inverse[here, :at] = dot(own, inverse[here, :at], plain, EXACT)
        inverse[here, here] = own
        if end < n:
            inverse[here, end:] = jnp.zeros((LANES, n - end), jnp.float32)
            right = dot(own, gram[here, end:], plain, EXACT)
            down_side = right.T
            gram[end:, end:] -= dot(down_side, right, plain, EXACT)
            moved = dot(down_side, inverse[here, :end], plain, EXACT)
            if at > 0:
                inverse[end:, :at] -= moved[:, :at]
            inverse[end:, here] = -moved[:, at:]
    scaled = inverse[...] * jnp.concatenate(across, axis=1)
    top = scaled.astype(jnp.bfloat16)
    high[...] = top
    low[...] = (scaled - top.astype(jnp.float32)).astype(jnp.bfloat16)


def factor(packed, pixels):
    n = 4 * LANES
    vmem = pl.BlockSpec(memory_space=pltpu.VMEM)
    return pl.pallas_call(
        functools.partial(factor_kernel, pixels),
        in_specs=[vmem],
        out_specs=[vmem, vmem, vmem],
        out_shape=[
            jax.ShapeDtypeStruct((n, n), jnp.bfloat16),
            jax.ShapeDtypeStruct((n, n), jnp.bfloat16),
            jax.ShapeDtypeStruct((1, n), jnp.float32),
        ],
        scratch_shapes=[pltpu.VMEM((n, n), jnp.float32), pltpu.VMEM((n, n), jnp.float32)],
        compiler_params=pltpu.CompilerParams(vmem_limit_bytes=VMEM_LIMIT),
        name="factor",
    )(packed)


def scores_kernel(high, low, factor_high, factor_low, out):
    half = 2 * LANES
    lanes = ((1,), (1,))
    for part in range(2):
        depth, cols = (part + 1) * half, slice(part * half, (part + 1) * half)
        a, al = high[:, :depth], low[:, :depth]
        f, fl = factor_high[cols, :depth], factor_low[cols, :depth]
        out[:, cols] = dot(a, f, lanes) + dot(al, f, lanes) + dot(a, fl, lanes)


def scores_of(high, low, factor_high, factor_low):
    pixels, n = high.shape
    tile = pl.BlockSpec((TILE, n), lambda t: (t, 0))
    whole = pl.BlockSpec((n, n), lambda t: (0, 0))
    return pl.pallas_call(
        scores_kernel,
        grid=(pixels // TILE,),
        in_specs=[tile, tile, whole, whole],
        out_specs=tile,
        out_shape=jax.ShapeDtypeStruct((pixels, n), jnp.float32),
        compiler_params=pltpu.CompilerParams(vmem_limit_bytes=VMEM_LIMIT),
        name="scores",
    )(high, low, factor_high, factor_low)


def shifted(value, axis, away):
    size = lax.axis_size(axis)
    return lax.ppermute(value, axis, [(k, (k + away) % size) for k in range(size)])


def swapped(value, axis, mask):
    return lax.ppermute(value, axis, [(k, k ^ mask) for k in range(lax.axis_size(axis))])


def summed(packed):
    core = lax.axis_index("core")
    blocks = packed.shape[0]
    half = packed.reshape(2, blocks // 2, LANES, LANES)
    mine = lax.dynamic_index_in_dim(half, core, 0, False)
    other = lax.dynamic_index_in_dim(half, 1 - core, 0, False)
    mine = mine + swapped(other, "core", 1)
    share = mine.reshape(16, -1, LANES)
    part = jnp.sum(lax.all_to_all(share, ("x", "z"), 0, 0), axis=0)
    part = swapped(part, "y", 1) + part
    part = swapped(part, "y", 2) + part
    spread = jnp.broadcast_to(part, share.shape)
    mine = lax.all_to_all(spread, ("x", "z"), 0, 0).reshape(mine.shape)
    other = swapped(mine, "core", 1)
    pair = jnp.where(core == 0, jnp.stack([mine, other]), jnp.stack([other, mine]))
    return pair.reshape(packed.shape)


def body(pixel_stack):
    y = lax.axis_index("y")
    lay = lax.axis_size("y")
    pixels = pixel_stack.shape[0] * 32
    blocks = pixel_stack.reshape(lay, -1, LANES)
    rows = blocks.shape[1] // CHUNKS
    arrived = []
    for chunk in range(CHUNKS):
        pieces = []
        for away in range(1, lay):
            sent = lax.dynamic_slice(
                blocks, (lax.rem(y + away, lay), chunk * rows, 0), (1, rows, LANES)
            ).reshape(rows, LANES)
            pieces.append(shifted(sent, "y", away))
        arrived.append(pieces)

    total = jnp.sum(pixel_stack, axis=0, keepdims=True)
    for axis, mask in (("core", 1), ("x", 1), ("x", 2), ("z", 1), ("z", 2)):
        total = total + swapped(total, axis, mask)
    mean = total / pixels
    means = jnp.zeros((1, lay * LANES), jnp.float32)
    for away in range(lay):
        value = mean if away == 0 else shifted(mean, "y", away)
        means = lax.dynamic_update_slice(means, value, (0, lax.rem(y - away + lay, lay) * LANES))

    place = y.astype(jnp.int32).reshape(1)
    carried = None
    for chunk in range(CHUNKS):
        *carried, packed = [
            *gram_chunk(chunk, place, blocks, arrived[chunk], means, carried),
            *([] if chunk == CHUNKS - 1 else [None]),
        ]
    high, low, _ = carried
    factor_high, factor_low, spread = factor(summed(packed), pixels)
    scores = scores_of(high, low, factor_high, factor_low)
    own = lax.dynamic_slice(spread, (0, y * LANES), (1, LANES)).reshape(LANES)
    return scores, 0.5 * jnp.log(own + 1e-05)


def solution(mesh):
    devices = mesh.devices.reshape(4, 4, 2, 4)
    fine = Mesh(devices, ("x", "z", "core", "y"))
    return jax.shard_map(
        body,
        mesh=fine,
        in_specs=(P(("x", "z", "core"), "y"),),
        out_specs=(P(("x", "z", "core", "y"), None), P("y")),
        check_vma=False,
    )
```

time: 604 us -> 203 us (0.34); the launches traced: 594 us -> 201 us
  blocking collectives: 227 us -> 29 us
  other arithmetic: 142 us -> 5.23 us
  matrix products: 54.5 us -> 0 us
  waiting for transfers between devices: 127 us -> 72.8 us
  Pallas kernels: 0 us -> 42.7 us
  starting transfers between devices: 7.14 us -> 43.1 us
  local copies, waits for them, and re-layouts: 32.8 us -> 7.88 us
    psum x2 -> x0, blocking collectives: 129 us -> none  [the longest x1 66 us: body(): mean = lax.psum(jnp.sum(regrouped, axis=0), ('pix', 'lay')) / total]
    another operation x17 -> x0, other arithmetic: 119 us -> none  [the longest x14 78.7 us: body(): lower = jnp.linalg.cholesky(gram)]
    all_to_all x1 -> x2, blocking collectives: 98.3 us -> 29 us  [the longest x1 16.7 us: summed(): part = jnp.sum(lax.all_to_all(share, ('x', 'z'), 0, 0), axis=0)]
    ppermute x7 -> x18, waiting for transfers between devices: 127 us -> 72.8 us  [the longest x9 56.7 us: shifted(): lax.ppermute(value, axis, [(k, (k + away) % size) for k in range(size)])]
    dot_general x2 -> x0, matrix products: 46 us -> none  [the longest x1 29.7 us: body(): jnp.dot(standard, inverse.T, precision=lax.Precision.HIGHEST, preferred_e...]
    pallas_call x0 -> x4, Pallas kernels: none -> 42.7 us  [the longest x1 19.7 us: factor(): pl.pallas_call(functools.partial(factor_kernel, pixels), in_specs=[vmem],...]
    ppermute x7 -> x18, starting transfers between devices: 7.14 us -> 43.1 us  [the longest x9 30 us: shifted(): lax.ppermute(value, axis, [(k, (k + away) % size) for k in range(size)])]
    mul x3 -> x1, other arithmetic: 16.2 us -> 0.53 us  [body(): return (scores, 0.5 * jnp.log(own + 1e-05))]
  transfers between devices with their start and end apart: 7 -> 18, of which waited for: 7 -> 12; matrix products, arithmetic and copies ran while one was open for 3% -> 2% of each run, Pallas kernels for 0% -> 3%
where the time goes in v1:
time: 203 us; the launch traced here: 201 us
  waiting for transfers between devices  72.8 us (36%)
  starting transfers between devices  43.1 us (21%)
  Pallas kernels  42.7 us (21%)
  blocking collectives  29 us (14%)
  local copies, waits for them, and re-layouts  7.88 us (4%)
  other arithmetic  5.23 us (3%)
    ppermute x9, waiting for transfers between devices, shifted(): lax.ppermute(value, axis, [(k, (k + away) % size) for k in range(size)])  56.7 us
    ppermute x9, starting transfers between devices, shifted(): lax.ppermute(value, axis, [(k, (k + away) % size) for k in range(size)])  30 us
    pallas_call x1, Pallas kernels, factor(): pl.pallas_call(functools.partial(factor_kernel, pixels), in_specs=[vmem],...  19.7 us
    all_to_all x1, blocking collectives, summed(): part = jnp.sum(lax.all_to_all(share, ('x', 'z'), 0, 0), axis=0)  16.7 us
    ppermute x9, waiting for transfers between devices, swapped(): lax.ppermute(value, axis, [(k, k ^ mask) for k in range(lax.axis_size(axi...  16.2 us
    ppermute x9, starting transfers between devices, swapped(): lax.ppermute(value, axis, [(k, k ^ mask) for k in range(lax.axis_size(axi...  13.1 us
    pallas_call x2, Pallas kernels, gram_chunk(): pl.pallas_call(functools.partial(gram_kernel, last, first), grid_spec=plt...  12.5 us
    all_to_all x1, blocking collectives, summed(): mine = lax.all_to_all(spread, ('x', 'z'), 0, 0).reshape(mine.shape)  12.3 us
  transfers between devices with their start and end apart: 18, of which 12 were waited for; matrix products, arithmetic and copies ran while one was open for 2% of the time, Pallas kernels for 3%

profile of v1, /device:TPU:0, one launch (start us, length us, event | category | flops | bytes accessed | tf_op | source)
XLA Modules:
  0.0 201.4 jit_solution(4031555036017707580)
XLA Ops:
  0.7 5.6 %dynamic-slice_bitcast_fusion = (f32[2048,128]{1,0:T(8,128)}, f32[2048,128]{1,0:T(8,128)}, f32[2048,128]{1,0:T(8,128)}, f32[2048,128]{1,0:T(8,128)}, f32[2048,128]{1,0:T(8,128)}, /*index=5*/f32[2048,128]{1,0:T(8,128)}) fusion(f32[4,4096,128]{2,1,0:T(8,128)} %bitcast.31, s32[]{:T(128)S(6)} %select_n.48, s32[]{:T(128)S(6)} %select_n.47, s32[]{:T(128)S(6)} %select_n.46), kind=kLoop, calls=%fused_computation | loop fusion | bytes 12582924 | tf_op jit(solution)/shard_map/reshape | solution.py:265
  7.9 4.6 %reduce_sum.18 = f32[128]{0:T(128)S(1)} reduce(f32[16384,128]{1,0:T(8,128)} %param.1, f32[]{:T(128)} %constant.54.clone.1), dimensions={0}, to_apply=%region_0.0 | reduce | flops 2097024 | bytes 8389124 | tf_op jit(solution)/shard_map/reduce_sum | solution.py:269
  15.2 2.0 %collective-permute-done.4 = f32[1,128]{1,0:T(1,128)S(1)} collective-permute-done((f32[1,128]{1,0:T(1,128)S(1)}, f32[1,128]{1,0:T(1,128)S(1)}, u32[]{:S(2)}, u32[]{:S(2)}) %collective-permute-start.4) | collective-permute-done | bytes 544 | tf_op jit(solution)/shard_map/ppermute | solution.py:232
  17.2 3.0 %collective-permute-start.5 = (f32[1,128]{1,0:T(1,128)S(1)}, f32[1,128]{1,0:T(1,128)S(1)}, u32[]{:S(2)}, u32[]{:S(2)}) collective-permute-start(f32[1,128]{1,0:T(1,128)S(1)} %add.100), channel_id=1, source_target_pairs={{0,64},{32,96},{64,0},{96,32},{1,65},{33,97},{65,1},{97,33},{2,66}... | collective-permute-start | bytes 1544 | tf_op jit(solution)/shard_map/ppermute | solution.py:232
  20.3 2.0 %collective-permute-done.5 = f32[1,128]{1,0:T(1,128)S(1)} collective-permute-done((f32[1,128]{1,0:T(1,128)S(1)}, f32[1,128]{1,0:T(1,128)S(1)}, u32[]{:S(2)}, u32[]{:S(2)}) %collective-permute-start.5) | collective-permute-done | bytes 544 | tf_op jit(solution)/shard_map/ppermute | solution.py:232
  22.3 1.9 collective-permute-start.6
  24.2 2.9 %collective-permute-start.12 = (f32[2048,128]{1,0:T(8,128)}, f32[2048,128]{1,0:T(8,128)S(1)}, u32[]{:S(2)}, u32[]{:S(2)}) collective-permute-start(f32[2048,128]{1,0:T(8,128)} %get-tuple-element.23), channel_id=1, source_target_pairs={{0,2},{1,3},{2,0},{3,1},{4,6},{5,7},{6,4},{7,5},{8,10},{9,11},{10,... | collective-permute-start | bytes 3145736 | tf_op jit(solution)/shard_map/ppermute | solution.py:228
  28.5 3.6 %collective-permute-start.7 = (f32[1,128]{1,0:T(1,128)S(1)}, f32[1,128]{1,0:T(1,128)S(1)}, u32[]{:S(2)}, u32[]{:S(2)}) collective-permute-start(f32[1,128]{1,0:T(1,128)S(1)} %add.102), channel_id=1, source_target_pairs={{0,16},{8,24},{16,0},{24,8},{1,17},{9,25},{17,1},{25,9},{2,18},{10... | collective-permute-start | bytes 1544 | tf_op jit(solution)/shard_map/ppermute | solution.py:232
  35.2 18.0 %collective-permute-done.8 = f32[1,128]{1,0:T(1,128)S(1)} collective-permute-done((f32[1,128]{1,0:T(1,128)S(1)}, f32[1,128]{1,0:T(1,128)S(1)}, u32[]{:S(2)}, u32[]{:S(2)}) %collective-permute-start.8) | collective-permute-done | bytes 544 | tf_op jit(solution)/shard_map/ppermute | solution.py:228
  53.2 3.7 %collective-permute-start.10 = (f32[1,128]{1,0:T(1,128)S(1)}, f32[1,128]{1,0:T(1,128)S(1)}, u32[]{:S(2)}, u32[]{:S(2)}) collective-permute-start(f32[1,128]{1,0:T(1,128)S(1)} %get-tuple-element.21), channel_id=1, source_target_pairs={{0,3},{1,0},{2,1},{3,2},{4,7},{5,4},{6,5},{7,6},{8,11},{9,8},{10,9... | collective-permute-start | bytes 1544 | tf_op jit(solution)/shard_map/ppermute | solution.py:228
  56.9 16.0 %collective-permute-start = (f32[2048,128]{1,0:T(8,128)}, f32[2048,128]{1,0:T(8,128)}, u32[]{:S(2)}, u32[]{:S(2)}) collective-permute-start(f32[2048,128]{1,0:T(8,128)} %get-tuple-element.27), channel_id=1, source_target_pairs={{0,1},{1,2},{2,3},{3,0},{4,5},{5,6},{6,7},{7,4},{8,9},{9,10},{10,1... | collective-permute-start | bytes 3145736 | tf_op jit(solution)/shard_map/ppermute | solution.py:228
  75.7 5.4 %gram.2 = (bf16[4096,512]{1,0:T(8,128)(2,1)}, bf16[4096,512]{1,0:T(8,128)(2,1)}, f32[5,256,256]{2,1,0:T(8,128)S(1)}) custom-call(s32[1]{0:T(128)} %bitcast.place, f32[4,4096,128]{2,1,0:T(8,128)} %bitcast.32, f32[2048,128]{1,0:T(8,128)S(1)} %collective-permute-done.11.near, f32[2048,128]{1,0:T(8,128)S(1)} %collective-permute-done.12.far, ...), custom_call_target="tpu_custom_call" | custom-call | flops 1879048192 | bytes 8388608 | tf_op jit(solution)/shard_map/gram/pallas_call | solution.py:106
  81.2 15.8 %collective-permute-done.near = f32[2048,128]{1,0:T(8,128)} collective-permute-done((f32[2048,128]{1,0:T(8,128)}, f32[2048,128]{1,0:T(8,128)}, u32[]{:S(2)}, u32[]{:S(2)}) %collective-permute-start) | collective-permute-done | bytes 1048608 | tf_op jit(solution)/shard_map/ppermute | solution.py:228
  96.9 20.1 %collective-permute-done.1.far = f32[2048,128]{1,0:T(8,128)} collective-permute-done((f32[2048,128]{1,0:T(8,128)}, f32[2048,128]{1,0:T(8,128)}, u32[]{:S(2)}, u32[]{:S(2)}) %collective-permute-start.1) | collective-permute-done | bytes 1048608 | tf_op jit(solution)/shard_map/ppermute | solution.py:228
  117.1 2.7 %collective-permute-done.2.back = f32[2048,128]{1,0:T(8,128)} collective-permute-done((f32[2048,128]{1,0:T(8,128)}, f32[2048,128]{1,0:T(8,128)}, u32[]{:S(2)}, u32[]{:S(2)}) %collective-permute-start.2) | collective-permute-done | bytes 1048608 | tf_op jit(solution)/shard_map/ppermute | solution.py:228
  119.8 7.0 %gram.3 = (bf16[4096,512]{1,0:T(8,128)(2,1)}, bf16[4096,512]{1,0:T(8,128)(2,1)}, f32[5,256,256]{2,1,0:T(8,128)S(1)}, f32[10,128,128]{2,1,0:T(8,128)S(1)}) custom-call(s32[1]{0:T(128)} %bitcast.place, f32[4,4096,128]{2,1,0:T(8,128)} %bitcast.33, f32[2048,128]{1,0:T(8,128)} %collective-permute-done.near, ...), custom_call_target="tpu_custom_call", output_to_operand_aliasing={{2}: (6, {}), {0}: (7, {}), {1}: (8, {})} | custom-call | flops 1879048192 | bytes 8388608 | tf_op jit(solution)/shard_map/gram/pallas_call | solution.py:106
  128.6 16.7 %all_to_all.10 = f32[16,40,128]{2,1,0:T(8,128)S(1)} all-to-all(f32[16,40,128]{2,1,0:T(8,128)S(1)} %bitcast.34), channel_id=1, replica_groups=mesh['x'=4,'z'=4,'core'=2,'y'=4] {'x','z'}, dimensions={0} | all-to-all | bytes 655360 | tf_op jit(solution)/shard_map/all_to_all | solution.py:243
  146.2 3.0 %collective-permute-done.15 = f32[40,128]{1,0:T(8,128)S(1)} collective-permute-done((f32[40,128]{1,0:T(8,128)S(1)}, f32[40,128]{1,0:T(8,128)S(1)}, u32[]{:S(2)}, u32[]{:S(2)}) %collective-permute-start.15) | collective-permute-done | bytes 20512 | tf_op jit(solution)/shard_map/ppermute | solution.py:232
  149.2 2.1 %collective-permute-start.16 = (f32[40,128]{1,0:T(8,128)S(1)}, f32[40,128]{1,0:T(8,128)S(1)}, u32[]{:S(2)}, u32[]{:S(2)}) collective-permute-start(f32[40,128]{1,0:T(8,128)S(1)} %add.112), channel_id=1, source_target_pairs={{0,2},{1,3},{2,0},{3,1},{4,6},{5,7},{6,4},{7,5},{8,10},{9,11},{10,... | collective-permute-start | bytes 61448 | tf_op jit(solution)/shard_map/ppermute | solution.py:232
  151.2 3.2 %collective-permute-done.16 = f32[40,128]{1,0:T(8,128)S(1)} collective-permute-done((f32[40,128]{1,0:T(8,128)S(1)}, f32[40,128]{1,0:T(8,128)S(1)}, u32[]{:S(2)}, u32[]{:S(2)}) %collective-permute-start.16) | collective-permute-done | bytes 20512 | tf_op jit(solution)/shard_map/ppermute | solution.py:232
  154.5 12.3 %all_to_all.11 = f32[16,40,128]{2,1,0:T(8,128)S(1)} all-to-all(f32[16,40,128]{2,1,0:T(8,128)S(1)} %broadcast_in_dim.11), channel_id=1, replica_groups=mesh['x'=4,'z'=4,'core'=2,'y'=4] {'x','z'}, dimensions={0} | all-to-all | bytes 655360 | tf_op jit(solution)/shard_map/all_to_all | solution.py:247
  168.5 19.7 %factor.1 = (bf16[512,512]{1,0:T(8,128)(2,1)S(1)}, bf16[512,512]{1,0:T(8,128)(2,1)S(1)}, f32[1,512]{1,0:T(1,128)S(1)}) custom-call(f32[10,128,128]{2,1,0:T(8,128)S(1)} %bitcast.28), custom_call_target="tpu_custom_call" | custom-call | tf_op jit(solution)/shard_map/factor/pallas_call | solution.py:186
  188.7 2.2 %copy-done = bf16[4096,512]{1,0:T(8,128)(2,1)S(1)} copy-done((bf16[4096,512]{1,0:T(8,128)(2,1)S(1)}, bf16[4096,512]{1,0:T(8,128)(2,1)}, u32[]{:S(2)}) %copy-start) | copy-done | bytes 4194328
  190.9 10.5 %scores.1 = f32[4096,512]{1,0:T(8,128)} custom-call(bf16[4096,512]{1,0:T(8,128)(2,1)S(1)} %copy-done, bf16[4096,512]{1,0:T(8,128)(2,1)} %get-tuple-element.15.low, bf16[512,512]{1,0:T(8,128)(2,1)S(1)} %get-tuple-element.17.factor_high, bf16[512,512]{1,0:T(8,128)(2,1)S(1)} %get-tuple-element.18.factor_low), custom_call_target="tpu_custom_call" | custom-call | tf_op jit(solution)/shard_map/scores/pallas_call | solution.py:215
  (39 shorter events, 16.4 us)
Async XLA Ops:
  6.3 68.3 %collective-permute-start.11 = (f32[2048,128]{1,0:T(8,128)}, f32[2048,128]{1,0:T(8,128)S(1)}, u32[]{:S(2)}, u32[]{:S(2)}) collective-permute-start(f32[2048,128]{1,0:T(8,128)} %get-tuple-element.24), channel_id=1, source_target_pairs={{0,1},{1,2},{2,3},{3,0},{4,5},{5,6},{6,7},{7,4},{8,9},{9,10},{10,1... | collective-permute-start | bytes 3145736 | tf_op jit(solution)/shard_map/ppermute | solution.py:228
  12.5 1.2 collective-permute-start.3
  13.7 3.5 %collective-permute-start.4 = (f32[1,128]{1,0:T(1,128)S(1)}, f32[1,128]{1,0:T(1,128)S(1)}, u32[]{:S(2)}, u32[]{:S(2)}) collective-permute-start(f32[1,128]{1,0:T(1,128)S(1)} %bitcast_add_fusion.1), channel_id=1, source_target_pairs={{0,32},{32,0},{64,96},{96,64},{1,33},{33,1},{65,97},{97,65},{2,34}... | collective-permute-start | bytes 1544 | tf_op jit(solution)/shard_map/ppermute | solution.py:232
  17.2 5.0 %collective-permute-start.5 = (f32[1,128]{1,0:T(1,128)S(1)}, f32[1,128]{1,0:T(1,128)S(1)}, u32[]{:S(2)}, u32[]{:S(2)}) collective-permute-start(f32[1,128]{1,0:T(1,128)S(1)} %add.100), channel_id=1, source_target_pairs={{0,64},{32,96},{64,0},{96,32},{1,65},{33,97},{65,1},{97,33},{2,66}... | collective-permute-start | bytes 1544 | tf_op jit(solution)/shard_map/ppermute | solution.py:232
  22.3 6.2 %collective-permute-start.6 = (f32[1,128]{1,0:T(1,128)S(1)}, f32[1,128]{1,0:T(1,128)S(1)}, u32[]{:S(2)}, u32[]{:S(2)}) collective-permute-start(f32[1,128]{1,0:T(1,128)S(1)} %add.101), channel_id=1, source_target_pairs={{0,8},{8,0},{16,24},{24,16},{1,9},{9,1},{17,25},{25,17},{2,10},{10... | collective-permute-start | bytes 1544 | tf_op jit(solution)/shard_map/ppermute | solution.py:232
  24.2 51.5 %collective-permute-start.12 = (f32[2048,128]{1,0:T(8,128)}, f32[2048,128]{1,0:T(8,128)S(1)}, u32[]{:S(2)}, u32[]{:S(2)}) collective-permute-start(f32[2048,128]{1,0:T(8,128)} %get-tuple-element.23), channel_id=1, source_target_pairs={{0,2},{1,3},{2,0},{3,1},{4,6},{5,7},{6,4},{7,5},{8,10},{9,11},{10,... | collective-permute-start | bytes 3145736 | tf_op jit(solution)/shard_map/ppermute | solution.py:228
  27.1 48.6 %collective-permute-start.13 = (f32[2048,128]{1,0:T(8,128)}, f32[2048,128]{1,0:T(8,128)S(1)}, u32[]{:S(2)}, u32[]{:S(2)}) collective-permute-start(f32[2048,128]{1,0:T(8,128)} %get-tuple-element.22), channel_id=1, source_target_pairs={{0,3},{1,0},{2,1},{3,2},{4,7},{5,4},{6,5},{7,6},{8,11},{9,8},{10,9... | collective-permute-start | bytes 3145736 | tf_op jit(solution)/shard_map/ppermute | solution.py:228
  28.5 5.1 %collective-permute-start.7 = (f32[1,128]{1,0:T(1,128)S(1)}, f32[1,128]{1,0:T(1,128)S(1)}, u32[]{:S(2)}, u32[]{:S(2)}) collective-permute-start(f32[1,128]{1,0:T(1,128)S(1)} %add.102), channel_id=1, source_target_pairs={{0,16},{8,24},{16,0},{24,8},{1,17},{9,25},{17,1},{25,9},{2,18},{10... | collective-permute-start | bytes 1544 | tf_op jit(solution)/shard_map/ppermute | solution.py:232
  33.6 19.6 %collective-permute-start.8 = (f32[1,128]{1,0:T(1,128)S(1)}, f32[1,128]{1,0:T(1,128)S(1)}, u32[]{:S(2)}, u32[]{:S(2)}) collective-permute-start(f32[1,128]{1,0:T(1,128)S(1)} %get-tuple-element.21), channel_id=1, source_target_pairs={{0,1},{1,2},{2,3},{3,0},{4,5},{5,6},{6,7},{7,4},{8,9},{9,10},{10,1... | collective-permute-start | bytes 1544 | tf_op jit(solution)/shard_map/ppermute | solution.py:228
  34.3 22.6 %collective-permute-start.9 = (f32[1,128]{1,0:T(1,128)S(1)}, f32[1,128]{1,0:T(1,128)S(1)}, u32[]{:S(2)}, u32[]{:S(2)}) collective-permute-start(f32[1,128]{1,0:T(1,128)S(1)} %get-tuple-element.21), channel_id=1, source_target_pairs={{0,2},{1,3},{2,0},{3,1},{4,6},{5,7},{6,4},{7,5},{8,10},{9,11},{10,... | collective-permute-start | bytes 1544 | tf_op jit(solution)/shard_map/ppermute | solution.py:228
  53.2 19.8 %collective-permute-start.10 = (f32[1,128]{1,0:T(1,128)S(1)}, f32[1,128]{1,0:T(1,128)S(1)}, u32[]{:S(2)}, u32[]{:S(2)}) collective-permute-start(f32[1,128]{1,0:T(1,128)S(1)} %get-tuple-element.21), channel_id=1, source_target_pairs={{0,3},{1,0},{2,1},{3,2},{4,7},{5,4},{6,5},{7,6},{8,11},{9,8},{10,9... | collective-permute-start | bytes 1544 | tf_op jit(solution)/shard_map/ppermute | solution.py:228
  56.9 40.0 %collective-permute-start = (f32[2048,128]{1,0:T(8,128)}, f32[2048,128]{1,0:T(8,128)}, u32[]{:S(2)}, u32[]{:S(2)}) collective-permute-start(f32[2048,128]{1,0:T(8,128)} %get-tuple-element.27), channel_id=1, source_target_pairs={{0,1},{1,2},{2,3},{3,0},{4,5},{5,6},{6,7},{7,4},{8,9},{9,10},{10,1... | collective-permute-start | bytes 3145736 | tf_op jit(solution)/shard_map/ppermute | solution.py:228
  73.0 44.1 %collective-permute-start.1 = (f32[2048,128]{1,0:T(8,128)}, f32[2048,128]{1,0:T(8,128)}, u32[]{:S(2)}, u32[]{:S(2)}) collective-permute-start(f32[2048,128]{1,0:T(8,128)} %get-tuple-element.26), channel_id=1, source_target_pairs={{0,2},{1,3},{2,0},{3,1},{4,6},{5,7},{6,4},{7,5},{8,10},{9,11},{10,... | collective-permute-start | bytes 3145736 | tf_op jit(solution)/shard_map/ppermute | solution.py:228
  74.5 45.2 %collective-permute-start.2 = (f32[2048,128]{1,0:T(8,128)}, f32[2048,128]{1,0:T(8,128)}, u32[]{:S(2)}, u32[]{:S(2)}) collective-permute-start(f32[2048,128]{1,0:T(8,128)} %get-tuple-element.25), channel_id=1, source_target_pairs={{0,3},{1,0},{2,1},{3,2},{4,7},{5,4},{6,5},{7,6},{8,11},{9,8},{10,9... | collective-permute-start | bytes 3145736 | tf_op jit(solution)/shard_map/ppermute | solution.py:228
  126.8 1.7 collective-permute-start.14
  145.3 3.9 %collective-permute-start.15 = (f32[40,128]{1,0:T(8,128)S(1)}, f32[40,128]{1,0:T(8,128)S(1)}, u32[]{:S(2)}, u32[]{:S(2)}) collective-permute-start(f32[40,128]{1,0:T(8,128)S(1)} %reduce_sum.19), channel_id=1, source_target_pairs={{0,1},{1,0},{2,3},{3,2},{4,5},{5,4},{6,7},{7,6},{8,9},{9,8},{10,11... | collective-permute-start | bytes 61448 | tf_op jit(solution)/shard_map/ppermute | solution.py:232
  149.2 5.3 %collective-permute-start.16 = (f32[40,128]{1,0:T(8,128)S(1)}, f32[40,128]{1,0:T(8,128)S(1)}, u32[]{:S(2)}, u32[]{:S(2)}) collective-permute-start(f32[40,128]{1,0:T(8,128)S(1)} %add.112), channel_id=1, source_target_pairs={{0,2},{1,3},{2,0},{3,1},{4,6},{5,7},{6,4},{7,5},{8,10},{9,11},{10,... | collective-permute-start | bytes 61448 | tf_op jit(solution)/shard_map/ppermute | solution.py:232
  166.8 1.6 collective-permute-start.17
  188.7 2.2 %copy-start = (bf16[4096,512]{1,0:T(8,128)(2,1)S(1)}, bf16[4096,512]{1,0:T(8,128)(2,1)}, u32[]{:S(2)}) copy-start(bf16[4096,512]{1,0:T(8,128)(2,1)} %get-tuple-element.14.high) | copy-start | bytes 12582916

commit v2 on v1

--- a/solution.py
+++ b/solution.py
@@ -10,9 +10,9 @@
 
 EXACT = lax.Precision.HIGHEST
 LANES = 128
-CHUNKS = 2
+CHUNKS = (512, 512, 2560, 512)
 TILE = 512
-VMEM_LIMIT = 48 * 2**20
+VMEM_LIMIT = 56 * 2**20
 
 
 def dot(a, b, contract, precision=None):
@@ -72,11 +72,11 @@
 
 
 def gram_chunk(chunk, place, blocks, pieces, mean, carried):
-    rows = pieces[0].shape[0]
+    rows = CHUNKS[chunk]
     steps = rows // TILE
     pixels, width = blocks.shape[1], 4 * LANES
-    first, last = chunk == 0, chunk == CHUNKS - 1
-    at = chunk * steps
+    first, last = chunk == 0, chunk == len(CHUNKS) - 1
+    at = sum(CHUNKS[:chunk]) // TILE
     piece = pl.BlockSpec((TILE, LANES), lambda t, y: (t, 0))
     whole = pl.BlockSpec((5, 256, 256), lambda t, y: (0, 0, 0))
     half = pl.BlockSpec((TILE, width), lambda t, y: (t + at, 0))
@@ -118,7 +118,7 @@
     )(*args)
 
 
-def factor_block(rest, carried):
+def factor_block(rest, carried, beside):
     outs = []
     row = lax.broadcasted_iota(jnp.int32, (8, LANES), 0)
     for at in range(0, LANES, 8):
@@ -137,11 +137,20 @@
             carried = carried - weight * carried[j : j + 1, :]
         outs.append(carried[:8] * scale)
         rest, carried = rest[8:], carried[8:]
+        beside(at // 8)
     return jnp.concatenate(outs, axis=0)
 
 
-def factor_kernel(pixels, packed, high, low, spread, gram, inverse):
+def whiten_kernel(pixels, packed, high_hbm, low_hbm, scores_hbm, spread, *scratch):
+    high, low, out, gram, inverse, both, in_sems, out_sems = scratch
     n = gram.shape[0]
+    fetches = [
+        pltpu.make_async_copy(high_hbm, high, in_sems.at[0]),
+        pltpu.make_async_copy(low_hbm, low, in_sems.at[1]),
+    ]
+    for fetch in fetches:
+        fetch.start()
+
     shape = (LANES, LANES)
     eye = lax.broadcasted_iota(jnp.int32, shape, 0) == lax.broadcasted_iota(jnp.int32, shape, 1)
     across, down = [], []
@@ -157,16 +166,40 @@
         gram[i * LANES : (i + 1) * LANES, j * LANES : (j + 1) * LANES] = block
         if i != j:
             gram[j * LANES : (j + 1) * LANES, i * LANES : (i + 1) * LANES] = block.T
-    plain = ((1,), (0,))
-    for at in range(0, n, LANES):
+
+    plain, lanes = ((1,), (0,)), ((1,), (1,))
+    pieces = 16
+    rows = high.shape[0] // pieces
+    sends = []
+
+    def score(column, piece):
+        depth = (column + 1) * LANES
+        here = slice(piece * rows, (piece + 1) * rows)
+        cols = slice(column * LANES, (column + 1) * LANES)
+        wide = dot(high[here, :depth], both[:, :depth], lanes)
+        narrow = dot(low[here, :depth], both[:LANES, :depth], lanes)
+        out[here, cols] = wide[:, :LANES] + wide[:, LANES:] + narrow
+        if piece % 4 == 3:
+            done = slice((piece - 3) * rows, (piece + 1) * rows)
+            send = pltpu.make_async_copy(
+                out.at[done, cols], scores_hbm.at[done, cols], out_sems.at[len(sends)]
+            )
+            send.start()
+            sends.append(send)
+
+    for column in range(4):
+        at = column * LANES
         end = at + LANES
         here = slice(at, end)
-        own = factor_block(gram[here, here], jnp.where(eye, 1.0, 0.0))
+        if column == 1:
+            for fetch in fetches:
+                fetch.wait()
+        beside = (lambda piece: score(column - 1, piece)) if column else (lambda piece: None)
+        own = factor_block(gram[here, here], jnp.where(eye, 1.0, 0.0), beside)
         if at > 0:
             inverse[here, :at] = dot(own, inverse[here, :at], plain, EXACT)
         inverse[here, here] = own
         if end < n:
-            inverse[here, end:] = jnp.zeros((LANES, n - end), jnp.float32)
             right = dot(own, gram[here, end:], plain, EXACT)
             down_side = right.T
             gram[end:, end:] -= dot(down_side, right, plain, EXACT)
@@ -174,53 +207,40 @@
             if at > 0:
                 inverse[end:, :at] -= moved[:, :at]
             inverse[end:, here] = -moved[:, at:]
-    scaled = inverse[...] * jnp.concatenate(across, axis=1)
-    top = scaled.astype(jnp.bfloat16)
-    high[...] = top
-    low[...] = (scaled - top.astype(jnp.float32)).astype(jnp.bfloat16)
-
-
-def factor(packed, pixels):
-    n = 4 * LANES
-    vmem = pl.BlockSpec(memory_space=pltpu.VMEM)
+        scaled = inverse[here, :end] * jnp.concatenate(across[: column + 1], axis=1)
+        top = scaled.astype(jnp.bfloat16)
+        both[:LANES, :end] = top
+        both[LANES:, :end] = (scaled - top.astype(jnp.float32)).astype(jnp.bfloat16)
+    for piece in range(pieces):
+        score(3, piece)
+    for send in sends:
+        send.wait()
+
+
+def whiten(packed, high, low, pixels):
+    rows, n = high.shape
+    vmem, hbm = pl.BlockSpec(memory_space=pltpu.VMEM), pl.BlockSpec(memory_space=pl.ANY)
     return pl.pallas_call(
-        functools.partial(factor_kernel, pixels),
-        in_specs=[vmem],
-        out_specs=[vmem, vmem, vmem],
+        functools.partial(whiten_kernel, pixels),
+        in_specs=[vmem, hbm, hbm],
+        out_specs=[hbm, vmem],
         out_shape=[
-            jax.ShapeDtypeStruct((n, n), jnp.bfloat16),
-            jax.ShapeDtypeStruct((n, n), jnp.bfloat16),
+            jax.ShapeDtypeStruct((rows, n), jnp.float32),
             jax.ShapeDtypeStruct((1, n), jnp.float32),
         ],
-        scratch_shapes=[pltpu.VMEM((n, n), jnp.float32), pltpu.VMEM((n, n), jnp.float32)],
+        scratch_shapes=[
+            pltpu.VMEM((rows, n), jnp.bfloat16),
+            pltpu.VMEM((rows, n), jnp.bfloat16),
+            pltpu.VMEM((rows, n), jnp.float32),
+            pltpu.VMEM((n, n), jnp.float32),
+            pltpu.VMEM((n, n), jnp.float32),
+            pltpu.VMEM((2 * LANES, n), jnp.bfloat16),
+            pltpu.SemaphoreType.DMA((2,)),
+            pltpu.SemaphoreType.DMA((16,)),
+        ],
         compiler_params=pltpu.CompilerParams(vmem_limit_bytes=VMEM_LIMIT),
-        name="factor",
-    )(packed)
-
-
-def scores_kernel(high, low, factor_high, factor_low, out):
-    half = 2 * LANES
-    lanes = ((1,), (1,))
-    for part in range(2):
-        depth, cols = (part + 1) * half, slice(part * half, (part + 1) * half)
-        a, al = high[:, :depth], low[:, :depth]
-        f, fl = factor_high[cols, :depth], factor_low[cols, :depth]
-        out[:, cols] = dot(a, f, lanes) + dot(al, f, lanes) + dot(a, fl, lanes)
-
-
-def scores_of(high, low, factor_high, factor_low):
-    pixels, n = high.shape
-    tile = pl.BlockSpec((TILE, n), lambda t: (t, 0))
-    whole = pl.BlockSpec((n, n), lambda t: (0, 0))
-    return pl.pallas_call(
-        scores_kernel,
-        grid=(pixels // TILE,),
-        in_specs=[tile, tile, whole, whole],
-        out_specs=tile,
-        out_shape=jax.ShapeDtypeStruct((pixels, n), jnp.float32),
-        compiler_params=pltpu.CompilerParams(vmem_limit_bytes=VMEM_LIMIT),
-        name="scores",
-    )(high, low, factor_high, factor_low)
+        name="whiten",
+    )(packed, high, low)
 
 
 def shifted(value, axis, away):
@@ -255,36 +275,38 @@
     lay = lax.axis_size("y")
     pixels = pixel_stack.shape[0] * 32
     blocks = pixel_stack.reshape(lay, -1, LANES)
-    rows = blocks.shape[1] // CHUNKS
-    arrived = []
-    for chunk in range(CHUNKS):
-        pieces = []
-        for away in range(1, lay):
-            sent = lax.dynamic_slice(
-                blocks, (lax.rem(y + away, lay), chunk * rows, 0), (1, rows, LANES)
-            ).reshape(rows, LANES)
-            pieces.append(shifted(sent, "y", away))
-        arrived.append(pieces)
-
-    total = jnp.sum(pixel_stack, axis=0, keepdims=True)
-    for axis, mask in (("core", 1), ("x", 1), ("x", 2), ("z", 1), ("z", 2)):
-        total = total + swapped(total, axis, mask)
-    mean = total / pixels
-    means = jnp.zeros((1, lay * LANES), jnp.float32)
+
+    def picked(source, chunk, away):
+        rows = CHUNKS[chunk]
+        start = (lax.rem(y + away, lay), sum(CHUNKS[:chunk]), 0)
+        return lax.dynamic_slice(source, start, (1, rows, LANES)).reshape(rows, LANES)
+
+    first = [picked(blocks, 0, away) for away in range(1, lay)]
+    stack, _ = lax.optimization_barrier((pixel_stack, first))
+    arrived = [[shifted(piece, "y", away) for away, piece in enumerate(first, 1)]]
+    total = jnp.sum(stack, axis=0, keepdims=True)
+    tail = jnp.broadcast_to(total, (8, LANES))
+    pieces = [jnp.concatenate([picked(blocks, 1, away), tail], axis=0) for away in range(1, lay)]
+    arrived.append([shifted(piece, "y", away) for away, piece in enumerate(pieces, 1)])
+    for chunk in range(2, len(CHUNKS)):
+        later, arrived[chunk - 2] = lax.optimization_barrier((blocks, arrived[chunk - 2]))
+        arrived.append(
+            [shifted(picked(later, chunk, away), "y", away) for away in range(1, lay)]
+        )
+
+    sums = jnp.zeros((1, lay * LANES), jnp.float32)
     for away in range(lay):
-        value = mean if away == 0 else shifted(mean, "y", away)
-        means = lax.dynamic_update_slice(means, value, (0, lax.rem(y - away + lay, lay) * LANES))
+        value = total if away == 0 else arrived[1][away - 1][-8:-7]
+        sums = lax.dynamic_update_slice(sums, value, (0, lax.rem(y - away + lay, lay) * LANES))
+    sums = lax.all_to_all(jnp.broadcast_to(sums, (32, 1, lay * LANES)), ("x", "z", "core"), 0, 0)
+    means = jnp.sum(sums, axis=0) / pixels
 
     place = y.astype(jnp.int32).reshape(1)
     carried = None
-    for chunk in range(CHUNKS):
-        *carried, packed = [
-            *gram_chunk(chunk, place, blocks, arrived[chunk], means, carried),
-            *([] if chunk == CHUNKS - 1 else [None]),
-        ]
-    high, low, _ = carried
-    factor_high, factor_low, spread = factor(summed(packed), pixels)
-    scores = scores_of(high, low, factor_high, factor_low)
+    for chunk, pieces in enumerate(arrived):
+        carried = gram_chunk(chunk, place, blocks, pieces, means, carried)
+    high, low, _, packed = carried
+    scores, spread = whiten(summed(packed), high, low, pixels)
     own = lax.dynamic_slice(spread, (0, y * LANES), (1, LANES)).reshape(LANES)
     return scores, 0.5 * jnp.log(own + 1e-05)
 

time: 203 us -> 178 us (0.88)
  waiting for transfers between devices: 72.8 us -> 18.3 us
  starting transfers between devices: 43.1 us -> 59.4 us
  Pallas kernels: 42.7 us -> 47.1 us
  other arithmetic: 5.23 us -> 9.24 us
  local copies, waits for them, and re-layouts: 7.88 us -> 11.8 us
    ppermute x9 -> x12, waiting for transfers between devices: 56.7 us -> 9.66 us  [shifted(): lax.ppermute(value, axis, [(k, (k + away) % size) for k in range(size)])]
    ppermute x9 -> x12, starting transfers between devices: 30 us -> 47.4 us  [shifted(): lax.ppermute(value, axis, [(k, (k + away) % size) for k in range(size)])]
    ppermute x9 -> x4, starting transfers between devices: 13.1 us -> 3.81 us  [swapped(): lax.ppermute(value, axis, [(k, k ^ mask) for k in range(lax.axis_size(axi...]
    all_to_all x0 -> x1, starting transfers between devices: none -> 8.17 us  [body(): lax.all_to_all(jnp.broadcast_to(sums, (32, 1, lay * LANES)), ('x', 'z', '...]
    ppermute x9 -> x4, waiting for transfers between devices: 16.2 us -> 8.67 us  [swapped(): lax.ppermute(value, axis, [(k, k ^ mask) for k in range(lax.axis_size(axi...]
    pallas_call x2 -> x4, Pallas kernels: 12.5 us -> 19.2 us  [gram_chunk(): pl.pallas_call(functools.partial(gram_kernel, last, first), grid_spec=plt...]
    pallas_call x2 -> x1, Pallas kernels: 30.2 us -> 27.9 us  [whiten(): pl.pallas_call(functools.partial(whiten_kernel, pixels), in_specs=[vmem,...]
    reshape x1 -> x3, local copies, waits for them, and re-layouts: 5.62 us -> 7.83 us  [picked(): lax.dynamic_slice(source, start, (1, rows, LANES)).reshape(rows, LANES)]
  transfers between devices with their start and end apart: 18 -> 17, of which waited for: 12 -> 8; matrix products, arithmetic and copies ran while one was open for 2% -> 8% of each run, Pallas kernels for 3% -> 9%
where the time goes in v2:
time: 178 us; the launch traced here: 176 us
  starting transfers between devices  59.4 us (33%)
  Pallas kernels  47.1 us (26%)
  blocking collectives  29.4 us (17%)
  waiting for transfers between devices  18.3 us (10%)
  local copies, waits for them, and re-layouts  11.8 us (7%)
  other arithmetic  9.24 us (5%)
    ppermute x12, starting transfers between devices, shifted(): lax.ppermute(value, axis, [(k, (k + away) % size) for k in range(size)])  47.4 us
    pallas_call x1, Pallas kernels, whiten(): pl.pallas_call(functools.partial(whiten_kernel, pixels), in_specs=[vmem,...  27.9 us
    pallas_call x4, Pallas kernels, gram_chunk(): pl.pallas_call(functools.partial(gram_kernel, last, first), grid_spec=plt...  19.2 us
    all_to_all x1, blocking collectives, summed(): part = jnp.sum(lax.all_to_all(share, ('x', 'z'), 0, 0), axis=0)  17.1 us
    all_to_all x1, blocking collectives, summed(): mine = lax.all_to_all(spread, ('x', 'z'), 0, 0).reshape(mine.shape)  12.3 us
    ppermute x12, waiting for transfers between devices, shifted(): lax.ppermute(value, axis, [(k, (k + away) % size) for k in range(size)])  9.66 us
    ppermute x4, waiting for transfers between devices, swapped(): lax.ppermute(value, axis, [(k, k ^ mask) for k in range(lax.axis_size(axi...  8.67 us
    all_to_all x1, starting transfers between devices, body(): lax.all_to_all(jnp.broadcast_to(sums, (32, 1, lay * LANES)), ('x', 'z', '...  8.17 us
  transfers between devices with their start and end apart: 17, of which 8 were waited for; matrix products, arithmetic and copies ran while one was open for 8% of the time, Pallas kernels for 9%

profile of v2, /device:TPU:0, one launch (start us, length us, event | category | flops | bytes accessed | tf_op | source)
XLA Modules:
  0.0 176.0 jit_solution(1685323278950220850)
XLA Ops:
  3.8 2.9 %collective-permute-start.7 = (f32[512,128]{1,0:T(8,128)S(1)}, f32[512,128]{1,0:T(8,128)S(1)}, u32[]{:S(2)}, u32[]{:S(2)}) collective-permute-start(f32[512,128]{1,0:T(8,128)S(1)} %get-tuple-element.57), channel_id=1, source_target_pairs={{0,2},{1,3},{2,0},{3,1},{4,6},{5,7},{6,4},{7,5},{8,10},{9,11},{10,... | collective-permute-start | bytes 786440 | tf_op jit(solution)/shard_map/ppermute | solution.py:248
  8.1 4.6 %reduce_sum.27 = f32[128]{0:T(128)S(1)} reduce(f32[16384,128]{1,0:T(8,128)} %param.1, f32[]{:T(128)} %constant.61.clone.1), dimensions={0}, to_apply=%region_0.0 | reduce | flops 2097024 | bytes 8389124 | tf_op jit(solution)/shard_map/reduce_sum | solution.py:287
  15.0 1.9 %collective-permute-start.2 = (f32[520,128]{1,0:T(8,128)}, f32[520,128]{1,0:T(8,128)S(1)}, u32[]{:S(2)}, u32[]{:S(2)}) collective-permute-start(f32[520,128]{1,0:T(8,128)} %get-tuple-element.60), channel_id=1, source_target_pairs={{0,3},{1,0},{2,1},{3,2},{4,7},{5,4},{6,5},{7,6},{8,11},{9,8},{10,9... | collective-permute-start | bytes 798728 | tf_op jit(solution)/shard_map/ppermute | solution.py:248
  16.9 2.6 %collective-permute-done.7.far = f32[512,128]{1,0:T(8,128)S(1)} collective-permute-done((f32[512,128]{1,0:T(8,128)S(1)}, f32[512,128]{1,0:T(8,128)S(1)}, u32[]{:S(2)}, u32[]{:S(2)}) %collective-permute-start.7) | collective-permute-done | bytes 262176 | tf_op jit(solution)/shard_map/ppermute | solution.py:248
  19.5 4.3 %dynamic-slice_bitcast_fusion = (f32[2560,128]{1,0:T(8,128)}, f32[2560,128]{1,0:T(8,128)}, f32[2560,128]{1,0:T(8,128)}) fusion(f32[4,4096,128]{2,1,0:T(8,128)} %bitcast.46, s32[]{:T(128)S(6)} %select_n.55, s32[]{:T(128)S(6)} %select_n.54, s32[]{:T(128)S(6)} %select_n.53), kind=kLoop, calls=%fused_computation | loop fusion | bytes 7864332 | tf_op jit(solution)/shard_map/reshape | solution.py:282
  23.8 2.7 %collective-permute-start.10 = (f32[2560,128]{1,0:T(8,128)}, f32[2560,128]{1,0:T(8,128)S(1)}, u32[]{:S(2)}, u32[]{:S(2)}) collective-permute-start(f32[2560,128]{1,0:T(8,128)} %get-tuple-element.49), channel_id=1, source_target_pairs={{0,2},{1,3},{2,0},{3,1},{4,6},{5,7},{6,4},{7,5},{8,10},{9,11},{10,... | collective-permute-start | bytes 3932168 | tf_op jit(solution)/shard_map/ppermute | solution.py:248
  26.6 2.0 %collective-permute-start.11 = (f32[2560,128]{1,0:T(8,128)}, f32[2560,128]{1,0:T(8,128)S(1)}, u32[]{:S(2)}, u32[]{:S(2)}) collective-permute-start(f32[2560,128]{1,0:T(8,128)} %get-tuple-element.48), channel_id=1, source_target_pairs={{0,3},{1,0},{2,1},{3,2},{4,7},{5,4},{6,5},{7,6},{8,11},{9,8},{10,9... | collective-permute-start | bytes 3932168 | tf_op jit(solution)/shard_map/ppermute | solution.py:248
  28.9 2.2 %collective-permute-done.1.far = f32[520,128]{1,0:T(8,128)S(1)} collective-permute-done((f32[520,128]{1,0:T(8,128)}, f32[520,128]{1,0:T(8,128)S(1)}, u32[]{:S(2)}, u32[]{:S(2)}) %collective-permute-start.1) | collective-permute-done | bytes 266272 | tf_op jit(solution)/shard_map/ppermute | solution.py:248
  32.0 8.2 %all-to-all-start = ((f32[32,1,512]{2,1,0:T(1,128)}), f32[32,1,512]{2,1,0:T(1,128)S(1)}, u32[]{:S(2)}, u32[]{:S(2)}) async-start(f32[32,1,512]{2,1,0:T(1,128)} %broadcast_in_dim.14), calls=%async_computation | async-start | bytes 131072 | tf_op jit(solution)/shard_map/all_to_all | solution.py:301
  40.2 2.1 %dynamic-slice_bitcast_fusion.4 = (f32[512,128]{1,0:T(8,128)}, f32[512,128]{1,0:T(8,128)}, f32[512,128]{1,0:T(8,128)}) fusion(f32[4,4096,128]{2,1,0:T(8,128)} %bitcast.47, s32[]{:T(128)S(6)} %select_n.55, s32[]{:T(128)S(6)} %select_n.54, s32[]{:T(128)S(6)} %select_n.53), kind=kLoop, calls=%fused_computation.9 | loop fusion | bytes 1572876 | tf_op jit(solution)/shard_map/reshape | solution.py:282
  42.2 1.9 %collective-permute-start.3 = (f32[512,128]{1,0:T(8,128)}, f32[512,128]{1,0:T(8,128)}, u32[]{:S(2)}, u32[]{:S(2)}) collective-permute-start(f32[512,128]{1,0:T(8,128)} %get-tuple-element.53), channel_id=1, source_target_pairs={{0,1},{1,2},{2,3},{3,0},{4,5},{5,6},{6,7},{7,4},{8,9},{9,10},{10,1... | collective-permute-start | bytes 786440 | tf_op jit(solution)/shard_map/ppermute | solution.py:248
  44.2 27.2 %collective-permute-start.4 = (f32[512,128]{1,0:T(8,128)}, f32[512,128]{1,0:T(8,128)}, u32[]{:S(2)}, u32[]{:S(2)}) collective-permute-start(f32[512,128]{1,0:T(8,128)} %get-tuple-element.52), channel_id=1, source_target_pairs={{0,2},{1,3},{2,0},{3,1},{4,6},{5,7},{6,4},{7,5},{8,10},{9,11},{10,... | collective-permute-start | bytes 786440 | tf_op jit(solution)/shard_map/ppermute | solution.py:248
  72.1 3.3 %gram.4 = (bf16[4096,512]{1,0:T(8,128)(2,1)}, bf16[4096,512]{1,0:T(8,128)(2,1)}, f32[5,256,256]{2,1,0:T(8,128)}) custom-call(s32[1]{0:T(128)} %bitcast.place, f32[4,4096,128]{2,1,0:T(8,128)} %bitcast.48, f32[512,128]{1,0:T(8,128)} %copy-done.7, f32[512,128]{1,0:T(8,128)} %copy-done.8, f32[512,128]{1,0:T(8,128)} %copy-done.9, f32[1,512]{1,0:T(1,128)} %bitcast.59), custom_call_target="tpu_custom_call" | custom-call | flops 469762048 | bytes 2097152 | tf_op jit(solution)/shard_map/gram/pallas_call | solution.py:106
  75.4 4.1 %collective-permute-start.5 = (f32[512,128]{1,0:T(8,128)S(1)}, f32[512,128]{1,0:T(8,128)S(1)}, u32[]{:S(2)}, u32[]{:S(2)}) collective-permute-start(f32[512,128]{1,0:T(8,128)S(1)} %copy-done.6), channel_id=1, source_target_pairs={{0,3},{1,0},{2,1},{3,2},{4,7},{5,4},{6,5},{7,6},{8,11},{9,8},{10,9... | collective-permute-start | bytes 786440 | tf_op jit(solution)/shard_map/ppermute | solution.py:248
  79.5 3.7 %gram.5 = (bf16[4096,512]{1,0:T(8,128)(2,1)}, bf16[4096,512]{1,0:T(8,128)(2,1)}, f32[5,256,256]{2,1,0:T(8,128)}) custom-call(s32[1]{0:T(128)} %bitcast.place, f32[4,4096,128]{2,1,0:T(8,128)} %bitcast.49, f32[520,128]{1,0:T(8,128)} %copy-done.2, f32[520,128]{1,0:T(8,128)} %copy-done.3, ...), custom_call_target="tpu_custom_call", output_to_operand_aliasing={{2}: (6, {}), {0}: (7, {}), {1}: (8, {})} | custom-call | flops 469762048 | bytes 2097152 | tf_op jit(solution)/shard_map/gram/pallas_call | solution.py:106
  83.2 3.9 %collective-permute-done.11.back = f32[2560,128]{1,0:T(8,128)S(1)} collective-permute-done((f32[2560,128]{1,0:T(8,128)}, f32[2560,128]{1,0:T(8,128)S(1)}, u32[]{:S(2)}, u32[]{:S(2)}) %collective-permute-start.11) | collective-permute-done | bytes 1310752 | tf_op jit(solution)/shard_map/ppermute | solution.py:248
  88.2 8.2 %gram.6 = (bf16[4096,512]{1,0:T(8,128)(2,1)}, bf16[4096,512]{1,0:T(8,128)(2,1)}, f32[5,256,256]{2,1,0:T(8,128)}) custom-call(s32[1]{0:T(128)} %bitcast.place, f32[4,4096,128]{2,1,0:T(8,128)} %bitcast.50, f32[2560,128]{1,0:T(8,128)} %collective-permute-done.9.near, f32[2560,128]{1,0:T(8,128)} %copy-done, ...), custom_call_target="tpu_custom_call", output_to_operand_aliasing={{2}: (6, {}), {0}: (7, {}), {1}: (8, {})} | custom-call | flops 2348810240 | bytes 10485760 | tf_op jit(solution)/shard_map/gram/pallas_call | solution.py:106
  98.1 3.9 %gram.7 = (bf16[4096,512]{1,0:T(8,128)(2,1)}, bf16[4096,512]{1,0:T(8,128)(2,1)}, f32[5,256,256]{2,1,0:T(8,128)}, f32[10,128,128]{2,1,0:T(8,128)}) custom-call(s32[1]{0:T(128)} %bitcast.place, f32[4,4096,128]{2,1,0:T(8,128)} %bitcast.51, f32[512,128]{1,0:T(8,128)} %collective-permute-done.3.near, ...), custom_call_target="tpu_custom_call", output_to_operand_aliasing={{2}: (6, {}), {0}: (7, {}), {1}: (8, {})} | custom-call | flops 469762048 | bytes 2097152 | tf_op jit(solution)/shard_map/gram/pallas_call | solution.py:106
  105.7 17.1 %all_to_all.15 = f32[16,40,128]{2,1,0:T(8,128)S(1)} all-to-all(f32[16,40,128]{2,1,0:T(8,128)S(1)} %bitcast.53), channel_id=1, replica_groups=mesh['x'=4,'z'=4,'core'=2,'y'=4] {'x','z'}, dimensions={0} | all-to-all | bytes 655360 | tf_op jit(solution)/shard_map/all_to_all | solution.py:263
  124.0 2.7 %collective-permute-done.13 = f32[40,128]{1,0:T(8,128)S(1)} collective-permute-done((f32[40,128]{1,0:T(8,128)S(1)}, f32[40,128]{1,0:T(8,128)S(1)}, u32[]{:S(2)}, u32[]{:S(2)}) %collective-permute-start.13) | collective-permute-done | bytes 20512 | tf_op jit(solution)/shard_map/ppermute | solution.py:252
  126.7 2.6 %collective-permute-start.14 = (f32[40,128]{1,0:T(8,128)S(1)}, f32[40,128]{1,0:T(8,128)S(1)}, u32[]{:S(2)}, u32[]{:S(2)}) collective-permute-start(f32[40,128]{1,0:T(8,128)S(1)} %add.104), channel_id=1, source_target_pairs={{0,2},{1,3},{2,0},{3,1},{4,6},{5,7},{6,4},{7,5},{8,10},{9,11},{10,... | collective-permute-start | bytes 61448 | tf_op jit(solution)/shard_map/ppermute | solution.py:252
  129.3 2.7 %collective-permute-done.14 = f32[40,128]{1,0:T(8,128)S(1)} collective-permute-done((f32[40,128]{1,0:T(8,128)S(1)}, f32[40,128]{1,0:T(8,128)S(1)}, u32[]{:S(2)}, u32[]{:S(2)}) %collective-permute-start.14) | collective-permute-done | bytes 20512 | tf_op jit(solution)/shard_map/ppermute | solution.py:252
  132.0 12.3 %all_to_all.16 = f32[16,40,128]{2,1,0:T(8,128)S(1)} all-to-all(f32[16,40,128]{2,1,0:T(8,128)S(1)} %broadcast_in_dim.15), channel_id=1, replica_groups=mesh['x'=4,'z'=4,'core'=2,'y'=4] {'x','z'}, dimensions={0} | all-to-all | bytes 655360 | tf_op jit(solution)/shard_map/all_to_all | solution.py:267
  146.9 27.9 %whiten.1 = (f32[4096,512]{1,0:T(8,128)}, f32[1,512]{1,0:T(1,128)}) custom-call(f32[10,128,128]{2,1,0:T(8,128)} %bitcast.52, bf16[4096,512]{1,0:T(8,128)(2,1)} %get-tuple-element.44.high_hbm, bf16[4096,512]{1,0:T(8,128)(2,1)} %get-tuple-element.45.low_hbm), custom_call_target="tpu_custom_call" | custom-call | tf_op jit(solution)/shard_map/whiten/pallas_call | solution.py:223
  (59 shorter events, 20.2 us)
Async XLA Ops:
  2.1 12.9 %collective-permute-start.6 = (f32[512,128]{1,0:T(8,128)S(1)}, f32[512,128]{1,0:T(8,128)S(1)}, u32[]{:S(2)}, u32[]{:S(2)}) collective-permute-start(f32[512,128]{1,0:T(8,128)S(1)} %get-tuple-element.58), channel_id=1, source_target_pairs={{0,1},{1,2},{2,3},{3,0},{4,5},{5,6},{6,7},{7,4},{8,9},{9,10},{10,1... | collective-permute-start | bytes 786440 | tf_op jit(solution)/shard_map/ppermute | solution.py:248
  3.8 15.7 %collective-permute-start.7 = (f32[512,128]{1,0:T(8,128)S(1)}, f32[512,128]{1,0:T(8,128)S(1)}, u32[]{:S(2)}, u32[]{:S(2)}) collective-permute-start(f32[512,128]{1,0:T(8,128)S(1)} %get-tuple-element.57), channel_id=1, source_target_pairs={{0,2},{1,3},{2,0},{3,1},{4,6},{5,7},{6,4},{7,5},{8,10},{9,11},{10,... | collective-permute-start | bytes 786440 | tf_op jit(solution)/shard_map/ppermute | solution.py:248
  6.7 12.8 %collective-permute-start.8 = (f32[512,128]{1,0:T(8,128)S(1)}, f32[512,128]{1,0:T(8,128)S(1)}, u32[]{:S(2)}, u32[]{:S(2)}) collective-permute-start(f32[512,128]{1,0:T(8,128)S(1)} %get-tuple-element.56), channel_id=1, source_target_pairs={{0,3},{1,0},{2,1},{3,2},{4,7},{5,4},{6,5},{7,6},{8,11},{9,8},{10,9... | collective-permute-start | bytes 786440 | tf_op jit(solution)/shard_map/ppermute | solution.py:248
  13.5 15.0 %collective-permute-start = (f32[520,128]{1,0:T(8,128)S(1)}, f32[520,128]{1,0:T(8,128)S(1)}, u32[]{:S(2)}, u32[]{:S(2)}) collective-permute-start(f32[520,128]{1,0:T(8,128)S(1)} %get-tuple-element.62), channel_id=1, source_target_pairs={{0,1},{1,2},{2,3},{3,0},{4,5},{5,6},{6,7},{7,4},{8,9},{9,10},{10,1... | collective-permute-start | bytes 798728 | tf_op jit(solution)/shard_map/ppermute | solution.py:248
  14.2 16.8 %collective-permute-start.1 = (f32[520,128]{1,0:T(8,128)}, f32[520,128]{1,0:T(8,128)S(1)}, u32[]{:S(2)}, u32[]{:S(2)}) collective-permute-start(f32[520,128]{1,0:T(8,128)} %get-tuple-element.61), channel_id=1, source_target_pairs={{0,2},{1,3},{2,0},{3,1},{4,6},{5,7},{6,4},{7,5},{8,10},{9,11},{10,... | collective-permute-start | bytes 798728 | tf_op jit(solution)/shard_map/ppermute | solution.py:248
  15.0 11.6 %copy-start.7 = (f32[512,128]{1,0:T(8,128)}, f32[512,128]{1,0:T(8,128)S(1)}, u32[]{:S(2)}) copy-start(f32[512,128]{1,0:T(8,128)S(1)} %collective-permute-done.6.near) | copy-start | bytes 786436
  15.0 16.0 %collective-permute-start.2 = (f32[520,128]{1,0:T(8,128)}, f32[520,128]{1,0:T(8,128)S(1)}, u32[]{:S(2)}, u32[]{:S(2)}) collective-permute-start(f32[520,128]{1,0:T(8,128)} %get-tuple-element.60), channel_id=1, source_target_pairs={{0,3},{1,0},{2,1},{3,2},{4,7},{5,4},{6,5},{7,6},{8,11},{9,8},{10,9... | collective-permute-start | bytes 798728 | tf_op jit(solution)/shard_map/ppermute | solution.py:248
  19.5 7.1 %copy-start.8 = (f32[512,128]{1,0:T(8,128)}, f32[512,128]{1,0:T(8,128)S(1)}, u32[]{:S(2)}) copy-start(f32[512,128]{1,0:T(8,128)S(1)} %collective-permute-done.7.far) | copy-start | bytes 786436
  19.5 7.1 %copy-start.9 = (f32[512,128]{1,0:T(8,128)}, f32[512,128]{1,0:T(8,128)S(1)}, u32[]{:S(2)}) copy-start(f32[512,128]{1,0:T(8,128)S(1)} %collective-permute-done.8.back) | copy-start | bytes 786436
  23.8 51.6 %collective-permute-start.10 = (f32[2560,128]{1,0:T(8,128)}, f32[2560,128]{1,0:T(8,128)S(1)}, u32[]{:S(2)}, u32[]{:S(2)}) collective-permute-start(f32[2560,128]{1,0:T(8,128)} %get-tuple-element.49), channel_id=1, source_target_pairs={{0,2},{1,3},{2,0},{3,1},{4,6},{5,7},{6,4},{7,5},{8,10},{9,11},{10,... | collective-permute-start | bytes 3932168 | tf_op jit(solution)/shard_map/ppermute | solution.py:248
  26.6 60.5 %collective-permute-start.11 = (f32[2560,128]{1,0:T(8,128)}, f32[2560,128]{1,0:T(8,128)S(1)}, u32[]{:S(2)}, u32[]{:S(2)}) collective-permute-start(f32[2560,128]{1,0:T(8,128)} %get-tuple-element.48), channel_id=1, source_target_pairs={{0,3},{1,0},{2,1},{3,2},{4,7},{5,4},{6,5},{7,6},{8,11},{9,8},{10,9... | collective-permute-start | bytes 3932168 | tf_op jit(solution)/shard_map/ppermute | solution.py:248
  28.6 46.8 %copy-start.2 = (f32[520,128]{1,0:T(8,128)}, f32[520,128]{1,0:T(8,128)S(1)}, u32[]{:S(2)}) copy-start(f32[520,128]{1,0:T(8,128)S(1)} %collective-permute-done.near) | copy-start | bytes 798724
  28.6 58.5 %collective-permute-start.9 = (f32[2560,128]{1,0:T(8,128)}, f32[2560,128]{1,0:T(8,128)}, u32[]{:S(2)}, u32[]{:S(2)}) collective-permute-start(f32[2560,128]{1,0:T(8,128)} %get-tuple-element.50), channel_id=1, source_target_pairs={{0,1},{1,2},{2,3},{3,0},{4,5},{5,6},{6,7},{7,4},{8,9},{9,10},{10,1... | collective-permute-start | bytes 3932168 | tf_op jit(solution)/shard_map/ppermute | solution.py:248
  31.0 44.4 %copy-start.3 = (f32[520,128]{1,0:T(8,128)}, f32[520,128]{1,0:T(8,128)S(1)}, u32[]{:S(2)}) copy-start(f32[520,128]{1,0:T(8,128)S(1)} %collective-permute-done.1.far) | copy-start | bytes 798724
  31.0 44.4 %copy-start.4 = (f32[520,128]{1,0:T(8,128)}, f32[520,128]{1,0:T(8,128)S(1)}, u32[]{:S(2)}) copy-start(f32[520,128]{1,0:T(8,128)S(1)} %collective-permute-done.2.back) | copy-start | bytes 798724
  32.0 39.4 %all-to-all-start = ((f32[32,1,512]{2,1,0:T(1,128)}), f32[32,1,512]{2,1,0:T(1,128)S(1)}, u32[]{:S(2)}, u32[]{:S(2)}) async-start(f32[32,1,512]{2,1,0:T(1,128)} %broadcast_in_dim.14), calls=%async_computation | async-start | bytes 131072 | tf_op jit(solution)/shard_map/all_to_all | solution.py:301
  42.2 54.1 %collective-permute-start.3 = (f32[512,128]{1,0:T(8,128)}, f32[512,128]{1,0:T(8,128)}, u32[]{:S(2)}, u32[]{:S(2)}) collective-permute-start(f32[512,128]{1,0:T(8,128)} %get-tuple-element.53), channel_id=1, source_target_pairs={{0,1},{1,2},{2,3},{3,0},{4,5},{5,6},{6,7},{7,4},{8,9},{9,10},{10,1... | collective-permute-start | bytes 786440 | tf_op jit(solution)/shard_map/ppermute | solution.py:248
  44.2 53.2 %collective-permute-start.4 = (f32[512,128]{1,0:T(8,128)}, f32[512,128]{1,0:T(8,128)}, u32[]{:S(2)}, u32[]{:S(2)}) collective-permute-start(f32[512,128]{1,0:T(8,128)} %get-tuple-element.52), channel_id=1, source_target_pairs={{0,2},{1,3},{2,0},{3,1},{4,6},{5,7},{6,4},{7,5},{8,10},{9,11},{10,... | collective-permute-start | bytes 786440 | tf_op jit(solution)/shard_map/ppermute | solution.py:248
  75.4 7.8 %copy-start = (f32[2560,128]{1,0:T(8,128)}, f32[2560,128]{1,0:T(8,128)S(1)}, u32[]{:S(2)}) copy-start(f32[2560,128]{1,0:T(8,128)S(1)} %collective-permute-done.10.far) | copy-start | bytes 3932164
  75.4 21.9 %collective-permute-start.5 = (f32[512,128]{1,0:T(8,128)S(1)}, f32[512,128]{1,0:T(8,128)S(1)}, u32[]{:S(2)}, u32[]{:S(2)}) collective-permute-start(f32[512,128]{1,0:T(8,128)S(1)} %copy-done.6), channel_id=1, source_target_pairs={{0,3},{1,0},{2,1},{3,2},{4,7},{5,4},{6,5},{7,6},{8,11},{9,8},{10,9... | collective-permute-start | bytes 786440 | tf_op jit(solution)/shard_map/ppermute | solution.py:248
  103.0 1.7 collective-permute-start.12
  122.8 3.9 %collective-permute-start.13 = (f32[40,128]{1,0:T(8,128)S(1)}, f32[40,128]{1,0:T(8,128)S(1)}, u32[]{:S(2)}, u32[]{:S(2)}) collective-permute-start(f32[40,128]{1,0:T(8,128)S(1)} %reduce_sum.29), channel_id=1, source_target_pairs={{0,1},{1,0},{2,3},{3,2},{4,5},{5,4},{6,7},{7,6},{8,9},{9,8},{10,11... | collective-permute-start | bytes 61448 | tf_op jit(solution)/shard_map/ppermute | solution.py:252
  126.7 5.3 %collective-permute-start.14 = (f32[40,128]{1,0:T(8,128)S(1)}, f32[40,128]{1,0:T(8,128)S(1)}, u32[]{:S(2)}, u32[]{:S(2)}) collective-permute-start(f32[40,128]{1,0:T(8,128)S(1)} %add.104), channel_id=1, source_target_pairs={{0,2},{1,3},{2,0},{3,1},{4,6},{5,7},{6,4},{7,5},{8,10},{9,11},{10,... | collective-permute-start | bytes 61448 | tf_op jit(solution)/shard_map/ppermute | solution.py:252
  144.3 1.6 collective-permute-start.15
  (3 other events, 5.1 us)

commit v3 on v2

--- a/solution.py
+++ b/solution.py
@@ -12,6 +12,7 @@
 LANES = 128
 CHUNKS = (512, 512, 2560, 512)
 TILE = 512
+PANEL = 64
 VMEM_LIMIT = 56 * 2**20
 
 
@@ -27,7 +28,7 @@
     if not first:
         rest.pop(0), rest.pop(0)
     high, low, sums = rest[:3]
-    packed = rest[3] if last else None
+    mine, other = rest[3:] if last else (None, None)
     step = pl.program_id(0)
 
     @pl.when(step == 0)
@@ -56,6 +57,7 @@
 
         @pl.when(step == pl.num_programs(0) - 1)
         def _():
+            packed = {}
             for side in range(2):
                 cross = sums[3 + side]
                 whole = sums[side] + cross + cross.T
@@ -66,6 +68,10 @@
             packed[4] = sums[2, LANES:, :LANES]
             packed[8] = sums[2, :LANES, LANES:]
             packed[9] = sums[2, LANES:, LANES:]
+            for block in range(5):
+                low_half = place[1] == 0
+                mine[block] = jnp.where(low_half, packed[block], packed[5 + block])
+                other[block] = jnp.where(low_half, packed[5 + block], packed[block])
 
 
 BLOCKS = ((0, 0), (1, 0), (1, 1), (2, 0), (3, 0), (2, 2), (3, 2), (3, 3), (2, 1), (3, 1))
@@ -101,8 +107,8 @@
         jax.ShapeDtypeStruct((5, 256, 256), jnp.float32),
     ]
     if last:
-        out_specs.append(pl.BlockSpec((10, LANES, LANES), lambda t, y: (0, 0, 0)))
-        out_shape.append(jax.ShapeDtypeStruct((10, LANES, LANES), jnp.float32))
+        out_specs += [pl.BlockSpec((5, LANES, LANES), lambda t, y: (0, 0, 0))] * 2
+        out_shape += [jax.ShapeDtypeStruct((5, LANES, LANES), jnp.float32)] * 2
     return pl.pallas_call(
         functools.partial(gram_kernel, last, first),
         grid_spec=pltpu.PrefetchScalarGridSpec(
@@ -118,30 +124,44 @@
     )(*args)
 
 
-def factor_block(rest, carried, beside):
-    outs = []
+def eliminate(rest, carried, first, beside):
+    kept, factor = [], []
     row = lax.broadcasted_iota(jnp.int32, (8, LANES), 0)
-    for at in range(0, LANES, 8):
-        rows = LANES - at
+    for at in range(first, first + PANEL, 8):
+        rows = rest.shape[0]
         columns = [jnp.broadcast_to(rest[:, at + c : at + c + 1], (rows, LANES)) for c in range(8)]
         scale = jnp.zeros((8, LANES), jnp.float32)
         for j in range(8):
-            pivot = columns[j][j : j + 1, :]
-            scale = jnp.where(row == j, lax.rsqrt(jnp.broadcast_to(pivot, (8, LANES))), scale)
-            weight = columns[j] * (1.0 / pivot)
+            root = lax.rsqrt(columns[j][j : j + 1, :])
+            scale = jnp.where(row == j, jnp.broadcast_to(root, (8, LANES)), scale)
+            weight = columns[j] * (root * root)
             inside = jnp.where(row > j, weight[:8], 0.0)
             weight = jnp.concatenate([inside, weight[8:]], axis=0) if rows > 8 else inside
             for c in range(j + 1, 8):
                 columns[c] = columns[c] - weight * columns[c][j : j + 1, :]
             rest = rest - weight * rest[j : j + 1, :]
             carried = carried - weight * carried[j : j + 1, :]
-        outs.append(carried[:8] * scale)
+        kept.append(rest[:8] * scale)
+        factor.append(carried[:8] * scale)
         rest, carried = rest[8:], carried[8:]
         beside(at // 8)
+    return jnp.concatenate(kept, axis=0), jnp.concatenate(factor, axis=0)
+
+
+def factor_block(rest, carried, beside):
+    outs = []
+    for first in range(0, LANES, PANEL):
+        kept, factor = eliminate(rest[:PANEL], carried[:PANEL], first, beside)
+        outs.append(factor)
+        if first + PANEL < LANES:
+            below = kept.T[first + PANEL :]
+            both = jnp.concatenate([kept, factor], axis=1)
+            moved = dot(below, both, ((1,), (0,)), EXACT)
+            rest, carried = rest[PANEL:] - moved[:, :LANES], carried[PANEL:] - moved[:, LANES:]
     return jnp.concatenate(outs, axis=0)
 
 
-def whiten_kernel(pixels, packed, high_hbm, low_hbm, scores_hbm, spread, *scratch):
+def whiten_kernel(pixels, place, mine, other, high_hbm, low_hbm, scores_hbm, log_scale, *scratch):
     high, low, out, gram, inverse, both, in_sems, out_sems = scratch
     n = gram.shape[0]
     fetches = [
@@ -151,22 +171,28 @@
     for fetch in fetches:
         fetch.start()
 
+    def packed(index):
+        side, block = divmod(index, 5)
+        return jnp.where(place[1] == side, mine[block], other[block])
+
     shape = (LANES, LANES)
     eye = lax.broadcasted_iota(jnp.int32, shape, 0) == lax.broadcasted_iota(jnp.int32, shape, 1)
     across, down = [], []
+    spread = jnp.zeros((1, LANES), jnp.float32)
     for k in range(4):
         index = BLOCKS.index((k, k))
-        diagonal = jnp.where(eye, packed[index], 0.0) * (1.0 / pixels)
+        diagonal = jnp.where(eye, packed(index), 0.0) * (1.0 / pixels)
         flat = jnp.sum(diagonal, axis=0, keepdims=True)
-        spread[0:1, k * LANES : (k + 1) * LANES] = flat
+        spread = spread + jnp.where(place[0] == k, flat, 0.0)
         across.append(lax.rsqrt(flat + 1e-05))
         down.append(lax.rsqrt(jnp.sum(diagonal, axis=1, keepdims=True) + 1e-05))
     for index, (i, j) in enumerate(BLOCKS):
-        block = packed[index] * (1.0 / pixels) * down[i] * across[j]
+        block = packed(index) * (1.0 / pixels) * down[i] * across[j]
         gram[i * LANES : (i + 1) * LANES, j * LANES : (j + 1) * LANES] = block
         if i != j:
             gram[j * LANES : (j + 1) * LANES, i * LANES : (i + 1) * LANES] = block.T
 
+    log_scale[...] = 0.5 * jnp.log(spread + 1e-05)
     plain, lanes = ((1,), (0,)), ((1,), (1,))
     pieces = 16
     rows = high.shape[0] // pieces
@@ -217,16 +243,16 @@
         send.wait()
 
 
-def whiten(packed, high, low, pixels):
+def whiten(place, mine, other, high, low, pixels):
     rows, n = high.shape
     vmem, hbm = pl.BlockSpec(memory_space=pltpu.VMEM), pl.BlockSpec(memory_space=pl.ANY)
     return pl.pallas_call(
         functools.partial(whiten_kernel, pixels),
-        in_specs=[vmem, hbm, hbm],
+        in_specs=[pl.BlockSpec(memory_space=pltpu.SMEM), vmem, vmem, hbm, hbm],
         out_specs=[hbm, vmem],
         out_shape=[
             jax.ShapeDtypeStruct((rows, n), jnp.float32),
-            jax.ShapeDtypeStruct((1, n), jnp.float32),
+            jax.ShapeDtypeStruct((1, LANES), jnp.float32),
         ],
         scratch_shapes=[
             pltpu.VMEM((rows, n), jnp.bfloat16),
@@ -240,7 +266,7 @@
         ],
         compiler_params=pltpu.CompilerParams(vmem_limit_bytes=VMEM_LIMIT),
         name="whiten",
-    )(packed, high, low)
+    )(place, mine, other, high, low)
 
 
 def shifted(value, axis, away):
@@ -252,12 +278,7 @@
     return lax.ppermute(value, axis, [(k, k ^ mask) for k in range(lax.axis_size(axis))])
 
 
-def summed(packed):
-    core = lax.axis_index("core")
-    blocks = packed.shape[0]
-    half = packed.reshape(2, blocks // 2, LANES, LANES)
-    mine = lax.dynamic_index_in_dim(half, core, 0, False)
-    other = lax.dynamic_index_in_dim(half, 1 - core, 0, False)
+def summed(mine, other):
     mine = mine + swapped(other, "core", 1)
     share = mine.reshape(16, -1, LANES)
     part = jnp.sum(lax.all_to_all(share, ("x", "z"), 0, 0), axis=0)
@@ -265,9 +286,7 @@
     part = swapped(part, "y", 2) + part
     spread = jnp.broadcast_to(part, share.shape)
     mine = lax.all_to_all(spread, ("x", "z"), 0, 0).reshape(mine.shape)
-    other = swapped(mine, "core", 1)
-    pair = jnp.where(core == 0, jnp.stack([mine, other]), jnp.stack([other, mine]))
-    return pair.reshape(packed.shape)
+    return mine, swapped(mine, "core", 1)
 
 
 def body(pixel_stack):
@@ -301,14 +320,14 @@
     sums = lax.all_to_all(jnp.broadcast_to(sums, (32, 1, lay * LANES)), ("x", "z", "core"), 0, 0)
     means = jnp.sum(sums, axis=0) / pixels
 
-    place = y.astype(jnp.int32).reshape(1)
+    place = jnp.stack([y, lax.axis_index("core")]).astype(jnp.int32)
     carried = None
     for chunk, pieces in enumerate(arrived):
         carried = gram_chunk(chunk, place, blocks, pieces, means, carried)
-    high, low, _, packed = carried
-    scores, spread = whiten(summed(packed), high, low, pixels)
-    own = lax.dynamic_slice(spread, (0, y * LANES), (1, LANES)).reshape(LANES)
-    return scores, 0.5 * jnp.log(own + 1e-05)
+    high, low, _, mine, other = carried
+    mine, other = summed(mine, other)
+    scores, log_scale = whiten(place, mine, other, high, low, pixels)
+    return scores, log_scale.reshape(LANES)
 
 
 def solution(mesh):

time: 178 us -> 175 us (0.983)
  waiting for transfers between devices: 18.3 us -> 15.2 us
    pallas_call x4, Pallas kernels: 19.2 us -> 21.9 us  [gram_chunk(): pl.pallas_call(functools.partial(gram_kernel, last, first), grid_spec=plt...]
    ppermute x12, waiting for transfers between devices: 9.66 us -> 7.01 us  [shifted(): lax.ppermute(value, axis, [(k, (k + away) % size) for k in range(size)])]
  transfers between devices with their start and end apart: 17 -> 17, of which waited for: 8 -> 8; matrix products, arithmetic and copies ran while one was open for 8% -> 8% of each run, Pallas kernels for 9% -> 10%
where the time goes in v3:
time: 175 us; the launch traced here: 173 us
  starting transfers between devices  60 us (34%)
  Pallas kernels  48.5 us (28%)
  blocking collectives  29.4 us (17%)
  waiting for transfers between devices  15.2 us (9%)
  local copies, waits for them, and re-layouts  11.6 us (7%)
  other arithmetic  7.71 us (4%)
    ppermute x12, starting transfers between devices, shifted(): lax.ppermute(value, axis, [(k, (k + away) % size) for k in range(size)])  47.4 us
    pallas_call x1, Pallas kernels, whiten(): pl.pallas_call(functools.partial(whiten_kernel, pixels), in_specs=[pl.Blo...  26.6 us
    pallas_call x4, Pallas kernels, gram_chunk(): pl.pallas_call(functools.partial(gram_kernel, last, first), grid_spec=plt...  21.9 us
    all_to_all x1, blocking collectives, summed(): part = jnp.sum(lax.all_to_all(share, ('x', 'z'), 0, 0), axis=0)  17.1 us
    all_to_all x1, blocking collectives, summed(): mine = lax.all_to_all(spread, ('x', 'z'), 0, 0).reshape(mine.shape)  12.3 us
    ppermute x4, waiting for transfers between devices, swapped(): lax.ppermute(value, axis, [(k, k ^ mask) for k in range(lax.axis_size(axi...  8.2 us
    all_to_all x1, starting transfers between devices, body(): lax.all_to_all(jnp.broadcast_to(sums, (32, 1, lay * LANES)), ('x', 'z', '...  8.16 us
    reshape x3, local copies, waits for them, and re-layouts, picked(): lax.dynamic_slice(source, start, (1, rows, LANES)).reshape(rows, LANES)  7.85 us
  transfers between devices with their start and end apart: 17, of which 8 were waited for; matrix products, arithmetic and copies ran while one was open for 8% of the time, Pallas kernels for 10%

profile of v3, /device:TPU:0, one launch (start us, length us, event | category | flops | bytes accessed | tf_op | source)
XLA Modules:
  0.0 173.3 jit_solution(6512599884846307492)
XLA Ops:
  3.8 2.9 %collective-permute-start.7 = (f32[512,128]{1,0:T(8,128)S(1)}, f32[512,128]{1,0:T(8,128)S(1)}, u32[]{:S(2)}, u32[]{:S(2)}) collective-permute-start(f32[512,128]{1,0:T(8,128)S(1)} %get-tuple-element.59), channel_id=1, source_target_pairs={{0,2},{1,3},{2,0},{3,1},{4,6},{5,7},{6,4},{7,5},{8,10},{9,11},{10,... | collective-permute-start | bytes 786440 | tf_op jit(solution)/shard_map/ppermute | solution.py:274
  8.1 4.6 %reduce_sum.27 = f32[128]{0:T(128)S(1)} reduce(f32[16384,128]{1,0:T(8,128)} %param.1, f32[]{:T(128)} %constant.52.clone.1), dimensions={0}, to_apply=%region_0.0 | reduce | flops 2097024 | bytes 8389124 | tf_op jit(solution)/shard_map/reduce_sum | solution.py:306
  15.0 1.9 %collective-permute-start.2 = (f32[520,128]{1,0:T(8,128)}, f32[520,128]{1,0:T(8,128)S(1)}, u32[]{:S(2)}, u32[]{:S(2)}) collective-permute-start(f32[520,128]{1,0:T(8,128)} %get-tuple-element.62), channel_id=1, source_target_pairs={{0,3},{1,0},{2,1},{3,2},{4,7},{5,4},{6,5},{7,6},{8,11},{9,8},{10,9... | collective-permute-start | bytes 798728 | tf_op jit(solution)/shard_map/ppermute | solution.py:274
  16.9 2.6 %collective-permute-done.7.far = f32[512,128]{1,0:T(8,128)S(1)} collective-permute-done((f32[512,128]{1,0:T(8,128)S(1)}, f32[512,128]{1,0:T(8,128)S(1)}, u32[]{:S(2)}, u32[]{:S(2)}) %collective-permute-start.7) | collective-permute-done | bytes 262176 | tf_op jit(solution)/shard_map/ppermute | solution.py:274
  19.5 4.3 %dynamic-slice_bitcast_fusion = (f32[2560,128]{1,0:T(8,128)}, f32[2560,128]{1,0:T(8,128)}, f32[2560,128]{1,0:T(8,128)}) fusion(f32[4,4096,128]{2,1,0:T(8,128)} %bitcast.38, s32[]{:T(128)S(6)} %select_n.32, s32[]{:T(128)S(6)} %select_n.15, s32[]{:T(128)S(6)} %select_n.14), kind=kLoop, calls=%fused_computation | loop fusion | bytes 7864332 | tf_op jit(solution)/shard_map/reshape | solution.py:301
  23.9 2.7 %collective-permute-start.10 = (f32[2560,128]{1,0:T(8,128)}, f32[2560,128]{1,0:T(8,128)S(1)}, u32[]{:S(2)}, u32[]{:S(2)}) collective-permute-start(f32[2560,128]{1,0:T(8,128)} %get-tuple-element.51), channel_id=1, source_target_pairs={{0,2},{1,3},{2,0},{3,1},{4,6},{5,7},{6,4},{7,5},{8,10},{9,11},{10,... | collective-permute-start | bytes 3932168 | tf_op jit(solution)/shard_map/ppermute | solution.py:274
  26.6 2.0 %collective-permute-start.11 = (f32[2560,128]{1,0:T(8,128)}, f32[2560,128]{1,0:T(8,128)S(1)}, u32[]{:S(2)}, u32[]{:S(2)}) collective-permute-start(f32[2560,128]{1,0:T(8,128)} %get-tuple-element.50), channel_id=1, source_target_pairs={{0,3},{1,0},{2,1},{3,2},{4,7},{5,4},{6,5},{7,6},{8,11},{9,8},{10,9... | collective-permute-start | bytes 3932168 | tf_op jit(solution)/shard_map/ppermute | solution.py:274
  32.0 8.2 %all-to-all-start = ((f32[32,1,512]{2,1,0:T(1,128)}), f32[32,1,512]{2,1,0:T(1,128)S(1)}, u32[]{:S(2)}, u32[]{:S(2)}) async-start(f32[32,1,512]{2,1,0:T(1,128)} %broadcast_in_dim.14), calls=%async_computation | async-start | bytes 131072 | tf_op jit(solution)/shard_map/all_to_all | solution.py:320
  40.2 2.1 %dynamic-slice_bitcast_fusion.3 = (f32[512,128]{1,0:T(8,128)}, f32[512,128]{1,0:T(8,128)}, f32[512,128]{1,0:T(8,128)}) fusion(f32[4,4096,128]{2,1,0:T(8,128)} %bitcast.39, s32[]{:T(128)S(6)} %select_n.32, s32[]{:T(128)S(6)} %select_n.15, s32[]{:T(128)S(6)} %select_n.14), kind=kLoop, calls=%fused_computation.6 | loop fusion | bytes 1572876 | tf_op jit(solution)/shard_map/reshape | solution.py:301
  42.2 1.9 %collective-permute-start.3 = (f32[512,128]{1,0:T(8,128)}, f32[512,128]{1,0:T(8,128)}, u32[]{:S(2)}, u32[]{:S(2)}) collective-permute-start(f32[512,128]{1,0:T(8,128)} %get-tuple-element.55), channel_id=1, source_target_pairs={{0,1},{1,2},{2,3},{3,0},{4,5},{5,6},{6,7},{7,4},{8,9},{9,10},{10,1... | collective-permute-start | bytes 786440 | tf_op jit(solution)/shard_map/ppermute | solution.py:274
  44.2 27.2 %collective-permute-start.4 = (f32[512,128]{1,0:T(8,128)}, f32[512,128]{1,0:T(8,128)}, u32[]{:S(2)}, u32[]{:S(2)}) collective-permute-start(f32[512,128]{1,0:T(8,128)} %get-tuple-element.54), channel_id=1, source_target_pairs={{0,2},{1,3},{2,0},{3,1},{4,6},{5,7},{6,4},{7,5},{8,10},{9,11},{10,... | collective-permute-start | bytes 786440 | tf_op jit(solution)/shard_map/ppermute | solution.py:274
  72.1 4.1 %gram.4 = (bf16[4096,512]{1,0:T(8,128)(2,1)}, bf16[4096,512]{1,0:T(8,128)(2,1)}, f32[5,256,256]{2,1,0:T(8,128)}) custom-call(s32[2]{0:T(128)} %pad_add_fusion.place, f32[4,4096,128]{2,1,0:T(8,128)} %bitcast.40, f32[512,128]{1,0:T(8,128)} %copy-done.9, f32[512,128]{1,0:T(8,128)} %copy-done.10, f32[512,128]{1,0:T(8,128)} %copy-done.11, f32[1,512]{1,0:T(1,128)} %bitcast.47), custom_call_target="tpu_custom_call" | custom-call | flops 469762048 | bytes 2097152 | tf_op jit(solution)/shard_map/gram/pallas_call | solution.py:112
  76.2 4.0 %collective-permute-start.5 = (f32[512,128]{1,0:T(8,128)S(1)}, f32[512,128]{1,0:T(8,128)S(1)}, u32[]{:S(2)}, u32[]{:S(2)}) collective-permute-start(f32[512,128]{1,0:T(8,128)S(1)} %copy-done.8), channel_id=1, source_target_pairs={{0,3},{1,0},{2,1},{3,2},{4,7},{5,4},{6,5},{7,6},{8,11},{9,8},{10,9... | collective-permute-start | bytes 786440 | tf_op jit(solution)/shard_map/ppermute | solution.py:274
  80.2 4.4 %gram.5 = (bf16[4096,512]{1,0:T(8,128)(2,1)}, bf16[4096,512]{1,0:T(8,128)(2,1)}, f32[5,256,256]{2,1,0:T(8,128)}) custom-call(s32[2]{0:T(128)} %pad_add_fusion.place, f32[4,4096,128]{2,1,0:T(8,128)} %bitcast.41, f32[520,128]{1,0:T(8,128)} %copy-done.4, f32[520,128]{1,0:T(8,128)} %copy-done.5, ...), custom_call_target="tpu_custom_call", output_to_operand_aliasing={{2}: (6, {}), {0}: (7, {}), {1}: (8, {})} | custom-call | flops 469762048 | bytes 2097152 | tf_op jit(solution)/shard_map/gram/pallas_call | solution.py:112
  84.6 2.5 %collective-permute-done.11.back = f32[2560,128]{1,0:T(8,128)S(1)} collective-permute-done((f32[2560,128]{1,0:T(8,128)}, f32[2560,128]{1,0:T(8,128)S(1)}, u32[]{:S(2)}, u32[]{:S(2)}) %collective-permute-start.11) | collective-permute-done | bytes 1310752 | tf_op jit(solution)/shard_map/ppermute | solution.py:274
  88.2 8.8 %gram.6 = (bf16[4096,512]{1,0:T(8,128)(2,1)}, bf16[4096,512]{1,0:T(8,128)(2,1)}, f32[5,256,256]{2,1,0:T(8,128)}) custom-call(s32[2]{0:T(128)} %pad_add_fusion.place, f32[4,4096,128]{2,1,0:T(8,128)} %bitcast.42, f32[2560,128]{1,0:T(8,128)} %collective-permute-done.9.near, ...), custom_call_target="tpu_custom_call", output_to_operand_aliasing={{2}: (6, {}), {0}: (7, {}), {1}: (8, {})} | custom-call | flops 2348810240 | bytes 10485760 | tf_op jit(solution)/shard_map/gram/pallas_call | solution.py:112
  98.1 4.6 %gram.7 = (bf16[4096,512]{1,0:T(8,128)(2,1)}, bf16[4096,512]{1,0:T(8,128)(2,1)}, f32[5,256,256]{2,1,0:T(8,128)}, f32[5,128,128]{2,1,0:T(8,128)}, f32[5,128,128]{2,1,0:T(8,128)}) custom-call(s32[2]{0:T(128)} %pad_add_fusion.place, f32[4,4096,128]{2,1,0:T(8,128)} %bitcast.43, ...), custom_call_target="tpu_custom_call", output_to_operand_aliasing={{2}: (6, {}), {0}: (7, {}), {1}: (8, {})} | custom-call | flops 469762048 | bytes 2097152 | tf_op jit(solution)/shard_map/gram/pallas_call | solution.py:112
  102.7 1.8 %collective-permute-done.12 = f32[5,128,128]{2,1,0:T(8,128)S(1)} collective-permute-done((f32[5,128,128]{2,1,0:T(8,128)}, f32[5,128,128]{2,1,0:T(8,128)S(1)}, u32[]{:S(2)}, u32[]{:S(2)}) %collective-permute-start.12) | collective-permute-done | bytes 327712 | tf_op jit(solution)/shard_map/ppermute | solution.py:278
  105.5 17.1 %all_to_all.15 = f32[16,40,128]{2,1,0:T(8,128)S(1)} all-to-all(f32[16,40,128]{2,1,0:T(8,128)S(1)} %bitcast.46), channel_id=1, replica_groups=mesh['x'=4,'z'=4,'core'=2,'y'=4] {'x','z'}, dimensions={0} | all-to-all | bytes 655360 | tf_op jit(solution)/shard_map/all_to_all | solution.py:284
  124.5 2.1 %collective-permute-done.13 = f32[40,128]{1,0:T(8,128)S(1)} collective-permute-done((f32[40,128]{1,0:T(8,128)S(1)}, f32[40,128]{1,0:T(8,128)S(1)}, u32[]{:S(2)}, u32[]{:S(2)}) %collective-permute-start.13) | collective-permute-done | bytes 20512 | tf_op jit(solution)/shard_map/ppermute | solution.py:278
  126.6 2.6 %collective-permute-start.14 = (f32[40,128]{1,0:T(8,128)S(1)}, f32[40,128]{1,0:T(8,128)S(1)}, u32[]{:S(2)}, u32[]{:S(2)}) collective-permute-start(f32[40,128]{1,0:T(8,128)S(1)} %add.84), channel_id=1, source_target_pairs={{0,2},{1,3},{2,0},{3,1},{4,6},{5,7},{6,4},{7,5},{8,10},{9,11},{10,... | collective-permute-start | bytes 61448 | tf_op jit(solution)/shard_map/ppermute | solution.py:278
  129.2 2.7 %collective-permute-done.14 = f32[40,128]{1,0:T(8,128)S(1)} collective-permute-done((f32[40,128]{1,0:T(8,128)S(1)}, f32[40,128]{1,0:T(8,128)S(1)}, u32[]{:S(2)}, u32[]{:S(2)}) %collective-permute-start.14) | collective-permute-done | bytes 20512 | tf_op jit(solution)/shard_map/ppermute | solution.py:278
  131.9 12.3 %all_to_all.16 = f32[16,40,128]{2,1,0:T(8,128)S(1)} all-to-all(f32[16,40,128]{2,1,0:T(8,128)S(1)} %broadcast_in_dim.15), channel_id=1, replica_groups=mesh['x'=4,'z'=4,'core'=2,'y'=4] {'x','z'}, dimensions={0} | all-to-all | bytes 655360 | tf_op jit(solution)/shard_map/all_to_all | solution.py:288
  146.6 26.6 %whiten.1 = (f32[4096,512]{1,0:T(8,128)}, f32[1,128]{1,0:T(1,128)}) custom-call(s32[2]{0:T(128)} %pad_add_fusion.place, f32[5,128,128]{2,1,0:T(8,128)} %bitcast.45, f32[5,128,128]{2,1,0:T(8,128)} %copy-done.3, bf16[4096,512]{1,0:T(8,128)(2,1)} %get-tuple-element.46.high_hbm, bf16[4096,512]{1,0:T(8,128)(2,1)} %get-tuple-element.47.low_hbm), custom_call_target="tpu_custom_call" | custom-call | tf_op jit(solution)/shard_map/whiten/pallas_call | solution.py:249
  (61 shorter events, 18.3 us)
Async XLA Ops:
  2.1 12.9 %collective-permute-start.6 = (f32[512,128]{1,0:T(8,128)S(1)}, f32[512,128]{1,0:T(8,128)S(1)}, u32[]{:S(2)}, u32[]{:S(2)}) collective-permute-start(f32[512,128]{1,0:T(8,128)S(1)} %get-tuple-element.60), channel_id=1, source_target_pairs={{0,1},{1,2},{2,3},{3,0},{4,5},{5,6},{6,7},{7,4},{8,9},{9,10},{10,1... | collective-permute-start | bytes 786440 | tf_op jit(solution)/shard_map/ppermute | solution.py:274
  3.8 15.7 %collective-permute-start.7 = (f32[512,128]{1,0:T(8,128)S(1)}, f32[512,128]{1,0:T(8,128)S(1)}, u32[]{:S(2)}, u32[]{:S(2)}) collective-permute-start(f32[512,128]{1,0:T(8,128)S(1)} %get-tuple-element.59), channel_id=1, source_target_pairs={{0,2},{1,3},{2,0},{3,1},{4,6},{5,7},{6,4},{7,5},{8,10},{9,11},{10,... | collective-permute-start | bytes 786440 | tf_op jit(solution)/shard_map/ppermute | solution.py:274
  6.7 12.8 %collective-permute-start.8 = (f32[512,128]{1,0:T(8,128)S(1)}, f32[512,128]{1,0:T(8,128)S(1)}, u32[]{:S(2)}, u32[]{:S(2)}) collective-permute-start(f32[512,128]{1,0:T(8,128)S(1)} %get-tuple-element.58), channel_id=1, source_target_pairs={{0,3},{1,0},{2,1},{3,2},{4,7},{5,4},{6,5},{7,6},{8,11},{9,8},{10,9... | collective-permute-start | bytes 786440 | tf_op jit(solution)/shard_map/ppermute | solution.py:274
  13.5 15.1 %collective-permute-start = (f32[520,128]{1,0:T(8,128)S(1)}, f32[520,128]{1,0:T(8,128)S(1)}, u32[]{:S(2)}, u32[]{:S(2)}) collective-permute-start(f32[520,128]{1,0:T(8,128)S(1)} %get-tuple-element.64), channel_id=1, source_target_pairs={{0,1},{1,2},{2,3},{3,0},{4,5},{5,6},{6,7},{7,4},{8,9},{9,10},{10,1... | collective-permute-start | bytes 798728 | tf_op jit(solution)/shard_map/ppermute | solution.py:274
  14.2 16.8 %collective-permute-start.1 = (f32[520,128]{1,0:T(8,128)}, f32[520,128]{1,0:T(8,128)S(1)}, u32[]{:S(2)}, u32[]{:S(2)}) collective-permute-start(f32[520,128]{1,0:T(8,128)} %get-tuple-element.63), channel_id=1, source_target_pairs={{0,2},{1,3},{2,0},{3,1},{4,6},{5,7},{6,4},{7,5},{8,10},{9,11},{10,... | collective-permute-start | bytes 798728 | tf_op jit(solution)/shard_map/ppermute | solution.py:274
  15.0 11.6 %copy-start.9 = (f32[512,128]{1,0:T(8,128)}, f32[512,128]{1,0:T(8,128)S(1)}, u32[]{:S(2)}) copy-start(f32[512,128]{1,0:T(8,128)S(1)} %collective-permute-done.6.near) | copy-start | bytes 786436
  15.0 16.0 %collective-permute-start.2 = (f32[520,128]{1,0:T(8,128)}, f32[520,128]{1,0:T(8,128)S(1)}, u32[]{:S(2)}, u32[]{:S(2)}) collective-permute-start(f32[520,128]{1,0:T(8,128)} %get-tuple-element.62), channel_id=1, source_target_pairs={{0,3},{1,0},{2,1},{3,2},{4,7},{5,4},{6,5},{7,6},{8,11},{9,8},{10,9... | collective-permute-start | bytes 798728 | tf_op jit(solution)/shard_map/ppermute | solution.py:274
  19.5 7.1 %copy-start.10 = (f32[512,128]{1,0:T(8,128)}, f32[512,128]{1,0:T(8,128)S(1)}, u32[]{:S(2)}) copy-start(f32[512,128]{1,0:T(8,128)S(1)} %collective-permute-done.7.far) | copy-start | bytes 786436
  19.5 7.1 %copy-start.11 = (f32[512,128]{1,0:T(8,128)}, f32[512,128]{1,0:T(8,128)S(1)}, u32[]{:S(2)}) copy-start(f32[512,128]{1,0:T(8,128)S(1)} %collective-permute-done.8.back) | copy-start | bytes 786436
  23.9 52.3 %collective-permute-start.10 = (f32[2560,128]{1,0:T(8,128)}, f32[2560,128]{1,0:T(8,128)S(1)}, u32[]{:S(2)}, u32[]{:S(2)}) collective-permute-start(f32[2560,128]{1,0:T(8,128)} %get-tuple-element.51), channel_id=1, source_target_pairs={{0,2},{1,3},{2,0},{3,1},{4,6},{5,7},{6,4},{7,5},{8,10},{9,11},{10,... | collective-permute-start | bytes 3932168 | tf_op jit(solution)/shard_map/ppermute | solution.py:274
  26.6 60.5 %collective-permute-start.11 = (f32[2560,128]{1,0:T(8,128)}, f32[2560,128]{1,0:T(8,128)S(1)}, u32[]{:S(2)}, u32[]{:S(2)}) collective-permute-start(f32[2560,128]{1,0:T(8,128)} %get-tuple-element.50), channel_id=1, source_target_pairs={{0,3},{1,0},{2,1},{3,2},{4,7},{5,4},{6,5},{7,6},{8,11},{9,8},{10,9... | collective-permute-start | bytes 3932168 | tf_op jit(solution)/shard_map/ppermute | solution.py:274
  28.6 47.6 %copy-start.4 = (f32[520,128]{1,0:T(8,128)}, f32[520,128]{1,0:T(8,128)S(1)}, u32[]{:S(2)}) copy-start(f32[520,128]{1,0:T(8,128)S(1)} %collective-permute-done.near) | copy-start | bytes 798724
  28.6 58.5 %collective-permute-start.9 = (f32[2560,128]{1,0:T(8,128)}, f32[2560,128]{1,0:T(8,128)}, u32[]{:S(2)}, u32[]{:S(2)}) collective-permute-start(f32[2560,128]{1,0:T(8,128)} %get-tuple-element.52), channel_id=1, source_target_pairs={{0,1},{1,2},{2,3},{3,0},{4,5},{5,6},{6,7},{7,4},{8,9},{9,10},{10,1... | collective-permute-start | bytes 3932168 | tf_op jit(solution)/shard_map/ppermute | solution.py:274
  31.0 45.1 %copy-start.5 = (f32[520,128]{1,0:T(8,128)}, f32[520,128]{1,0:T(8,128)S(1)}, u32[]{:S(2)}) copy-start(f32[520,128]{1,0:T(8,128)S(1)} %collective-permute-done.1.far) | copy-start | bytes 798724
  31.0 45.1 %copy-start.6 = (f32[520,128]{1,0:T(8,128)}, f32[520,128]{1,0:T(8,128)S(1)}, u32[]{:S(2)}) copy-start(f32[520,128]{1,0:T(8,128)S(1)} %collective-permute-done.2.back) | copy-start | bytes 798724
  32.0 39.4 %all-to-all-start = ((f32[32,1,512]{2,1,0:T(1,128)}), f32[32,1,512]{2,1,0:T(1,128)S(1)}, u32[]{:S(2)}, u32[]{:S(2)}) async-start(f32[32,1,512]{2,1,0:T(1,128)} %broadcast_in_dim.14), calls=%async_computation | async-start | bytes 131072 | tf_op jit(solution)/shard_map/all_to_all | solution.py:320
  42.2 54.8 %collective-permute-start.3 = (f32[512,128]{1,0:T(8,128)}, f32[512,128]{1,0:T(8,128)}, u32[]{:S(2)}, u32[]{:S(2)}) collective-permute-start(f32[512,128]{1,0:T(8,128)} %get-tuple-element.55), channel_id=1, source_target_pairs={{0,1},{1,2},{2,3},{3,0},{4,5},{5,6},{6,7},{7,4},{8,9},{9,10},{10,1... | collective-permute-start | bytes 786440 | tf_op jit(solution)/shard_map/ppermute | solution.py:274
  44.2 53.2 %collective-permute-start.4 = (f32[512,128]{1,0:T(8,128)}, f32[512,128]{1,0:T(8,128)}, u32[]{:S(2)}, u32[]{:S(2)}) collective-permute-start(f32[512,128]{1,0:T(8,128)} %get-tuple-element.54), channel_id=1, source_target_pairs={{0,2},{1,3},{2,0},{3,1},{4,6},{5,7},{6,4},{7,5},{8,10},{9,11},{10,... | collective-permute-start | bytes 786440 | tf_op jit(solution)/shard_map/ppermute | solution.py:274
  76.2 8.5 %copy-start = (f32[2560,128]{1,0:T(8,128)}, f32[2560,128]{1,0:T(8,128)S(1)}, u32[]{:S(2)}) copy-start(f32[2560,128]{1,0:T(8,128)S(1)} %collective-permute-done.10.far) | copy-start | bytes 3932164
  76.2 21.2 %collective-permute-start.5 = (f32[512,128]{1,0:T(8,128)S(1)}, f32[512,128]{1,0:T(8,128)S(1)}, u32[]{:S(2)}, u32[]{:S(2)}) collective-permute-start(f32[512,128]{1,0:T(8,128)S(1)} %copy-done.8), channel_id=1, source_target_pairs={{0,3},{1,0},{2,1},{3,2},{4,7},{5,4},{6,5},{7,6},{8,11},{9,8},{10,9... | collective-permute-start | bytes 786440 | tf_op jit(solution)/shard_map/ppermute | solution.py:274
  102.7 1.8 %collective-permute-start.12 = (f32[5,128,128]{2,1,0:T(8,128)}, f32[5,128,128]{2,1,0:T(8,128)S(1)}, u32[]{:S(2)}, u32[]{:S(2)}) collective-permute-start(f32[5,128,128]{2,1,0:T(8,128)} %get-tuple-element.45), channel_id=1, source_target_pairs={{0,4},{4,0},{1,5},{5,1},{2,6},{6,2},{3,7},{7,3},{8,12},{12,8},{9,1... | collective-permute-start | bytes 983048 | tf_op jit(solution)/shard_map/ppermute | solution.py:278
  122.7 3.9 %collective-permute-start.13 = (f32[40,128]{1,0:T(8,128)S(1)}, f32[40,128]{1,0:T(8,128)S(1)}, u32[]{:S(2)}, u32[]{:S(2)}) collective-permute-start(f32[40,128]{1,0:T(8,128)S(1)} %reduce_sum.29), channel_id=1, source_target_pairs={{0,1},{1,0},{2,3},{3,2},{4,5},{5,4},{6,7},{7,6},{8,9},{9,8},{10,11... | collective-permute-start | bytes 61448 | tf_op jit(solution)/shard_map/ppermute | solution.py:278
  126.6 5.3 %collective-permute-start.14 = (f32[40,128]{1,0:T(8,128)S(1)}, f32[40,128]{1,0:T(8,128)S(1)}, u32[]{:S(2)}, u32[]{:S(2)}) collective-permute-start(f32[40,128]{1,0:T(8,128)S(1)} %add.84), channel_id=1, source_target_pairs={{0,2},{1,3},{2,0},{3,1},{4,6},{5,7},{6,4},{7,5},{8,10},{9,11},{10,... | collective-permute-start | bytes 61448 | tf_op jit(solution)/shard_map/ppermute | solution.py:278
  144.2 1.6 collective-permute-start.15
  (5 other events, 8.3 us)

commit v4 on v3

--- a/solution.py
+++ b/solution.py
@@ -282,8 +282,8 @@
     mine = mine + swapped(other, "core", 1)
     share = mine.reshape(16, -1, LANES)
     part = jnp.sum(lax.all_to_all(share, ("x", "z"), 0, 0), axis=0)
-    part = swapped(part, "y", 1) + part
-    part = swapped(part, "y", 2) + part
+    beside, across, askew = (swapped(part, "y", mask) for mask in (1, 2, 3))
+    part = (part + beside) + (across + askew)
     spread = jnp.broadcast_to(part, share.shape)
     mine = lax.all_to_all(spread, ("x", "z"), 0, 0).reshape(mine.shape)
     return mine, swapped(mine, "core", 1)

time: 175 us -> 175 us (level)
    ppermute x4 -> x5, waiting for transfers between devices: 8.2 us -> 7.67 us  [swapped(): lax.ppermute(value, axis, [(k, k ^ mask) for k in range(lax.axis_size(axi...]
    ppermute x4 -> x5, starting transfers between devices: 4.41 us -> 4.78 us  [swapped(): lax.ppermute(value, axis, [(k, k ^ mask) for k in range(lax.axis_size(axi...]
  transfers between devices with their start and end apart: 17 -> 18, of which waited for: 8 -> 8; matrix products, arithmetic and copies ran while one was open for 8% -> 8% of each run, Pallas kernels for 10% -> 10%
where the time goes in v4:
time: 175 us; the launch traced here: 173 us
  starting transfers between devices  60.3 us (34%)
  Pallas kernels  48.5 us (28%)
  blocking collectives  29.4 us (17%)
  waiting for transfers between devices  14.7 us (8%)
  local copies, waits for them, and re-layouts  11.5 us (7%)
  other arithmetic  7.75 us (4%)
    ppermute x12, starting transfers between devices, shifted(): lax.ppermute(value, axis, [(k, (k + away) % size) for k in range(size)])  47.4 us
    pallas_call x1, Pallas kernels, whiten(): pl.pallas_call(functools.partial(whiten_kernel, pixels), in_specs=[pl.Blo...  26.6 us
    pallas_call x4, Pallas kernels, gram_chunk(): pl.pallas_call(functools.partial(gram_kernel, last, first), grid_spec=plt...  21.9 us
    all_to_all x1, blocking collectives, summed(): part = jnp.sum(lax.all_to_all(share, ('x', 'z'), 0, 0), axis=0)  17.1 us
    all_to_all x1, blocking collectives, summed(): mine = lax.all_to_all(spread, ('x', 'z'), 0, 0).reshape(mine.shape)  12.3 us
    all_to_all x1, starting transfers between devices, body(): lax.all_to_all(jnp.broadcast_to(sums, (32, 1, lay * LANES)), ('x', 'z', '...  8.16 us
    reshape x3, local copies, waits for them, and re-layouts, picked(): lax.dynamic_slice(source, start, (1, rows, LANES)).reshape(rows, LANES)  7.84 us
    ppermute x5, waiting for transfers between devices, swapped(): lax.ppermute(value, axis, [(k, k ^ mask) for k in range(lax.axis_size(axi...  7.67 us
  transfers between devices with their start and end apart: 18, of which 8 were waited for; matrix products, arithmetic and copies ran while one was open for 8% of the time, Pallas kernels for 10%

profile of v4, /device:TPU:0, one launch (start us, length us, event | category | flops | bytes accessed | tf_op | source)
XLA Modules:
  0.0 173.2 jit_solution(7396468863955086804)
XLA Ops:
  3.8 2.9 %collective-permute-start.7 = (f32[512,128]{1,0:T(8,128)S(1)}, f32[512,128]{1,0:T(8,128)S(1)}, u32[]{:S(2)}, u32[]{:S(2)}) collective-permute-start(f32[512,128]{1,0:T(8,128)S(1)} %get-tuple-element.59), channel_id=1, source_target_pairs={{0,2},{1,3},{2,0},{3,1},{4,6},{5,7},{6,4},{7,5},{8,10},{9,11},{10,... | collective-permute-start | bytes 786440 | tf_op jit(solution)/shard_map/ppermute | solution.py:274
  8.1 4.6 %reduce_sum.27 = f32[128]{0:T(128)S(1)} reduce(f32[16384,128]{1,0:T(8,128)} %param.1, f32[]{:T(128)} %constant.52.clone.1), dimensions={0}, to_apply=%region_0.0 | reduce | flops 2097024 | bytes 8389124 | tf_op jit(solution)/shard_map/reduce_sum | solution.py:306
  15.0 1.9 %collective-permute-start.2 = (f32[520,128]{1,0:T(8,128)}, f32[520,128]{1,0:T(8,128)S(1)}, u32[]{:S(2)}, u32[]{:S(2)}) collective-permute-start(f32[520,128]{1,0:T(8,128)} %get-tuple-element.62), channel_id=1, source_target_pairs={{0,3},{1,0},{2,1},{3,2},{4,7},{5,4},{6,5},{7,6},{8,11},{9,8},{10,9... | collective-permute-start | bytes 798728 | tf_op jit(solution)/shard_map/ppermute | solution.py:274
  16.9 2.6 %collective-permute-done.7.far = f32[512,128]{1,0:T(8,128)S(1)} collective-permute-done((f32[512,128]{1,0:T(8,128)S(1)}, f32[512,128]{1,0:T(8,128)S(1)}, u32[]{:S(2)}, u32[]{:S(2)}) %collective-permute-start.7) | collective-permute-done | bytes 262176 | tf_op jit(solution)/shard_map/ppermute | solution.py:274
  19.5 4.3 %dynamic-slice_bitcast_fusion = (f32[2560,128]{1,0:T(8,128)}, f32[2560,128]{1,0:T(8,128)}, f32[2560,128]{1,0:T(8,128)}) fusion(f32[4,4096,128]{2,1,0:T(8,128)} %bitcast.38, s32[]{:T(128)S(6)} %select_n.32, s32[]{:T(128)S(6)} %select_n.15, s32[]{:T(128)S(6)} %select_n.14), kind=kLoop, calls=%fused_computation | loop fusion | bytes 7864332 | tf_op jit(solution)/shard_map/reshape | solution.py:301
  23.8 2.7 %collective-permute-start.10 = (f32[2560,128]{1,0:T(8,128)}, f32[2560,128]{1,0:T(8,128)S(1)}, u32[]{:S(2)}, u32[]{:S(2)}) collective-permute-start(f32[2560,128]{1,0:T(8,128)} %get-tuple-element.51), channel_id=1, source_target_pairs={{0,2},{1,3},{2,0},{3,1},{4,6},{5,7},{6,4},{7,5},{8,10},{9,11},{10,... | collective-permute-start | bytes 3932168 | tf_op jit(solution)/shard_map/ppermute | solution.py:274
  26.6 2.0 %collective-permute-start.11 = (f32[2560,128]{1,0:T(8,128)}, f32[2560,128]{1,0:T(8,128)S(1)}, u32[]{:S(2)}, u32[]{:S(2)}) collective-permute-start(f32[2560,128]{1,0:T(8,128)} %get-tuple-element.50), channel_id=1, source_target_pairs={{0,3},{1,0},{2,1},{3,2},{4,7},{5,4},{6,5},{7,6},{8,11},{9,8},{10,9... | collective-permute-start | bytes 3932168 | tf_op jit(solution)/shard_map/ppermute | solution.py:274
  32.0 8.2 %all-to-all-start = ((f32[32,1,512]{2,1,0:T(1,128)}), f32[32,1,512]{2,1,0:T(1,128)S(1)}, u32[]{:S(2)}, u32[]{:S(2)}) async-start(f32[32,1,512]{2,1,0:T(1,128)} %broadcast_in_dim.14), calls=%async_computation | async-start | bytes 131072 | tf_op jit(solution)/shard_map/all_to_all | solution.py:320
  40.2 2.1 %dynamic-slice_bitcast_fusion.3 = (f32[512,128]{1,0:T(8,128)}, f32[512,128]{1,0:T(8,128)}, f32[512,128]{1,0:T(8,128)}) fusion(f32[4,4096,128]{2,1,0:T(8,128)} %bitcast.39, s32[]{:T(128)S(6)} %select_n.32, s32[]{:T(128)S(6)} %select_n.15, s32[]{:T(128)S(6)} %select_n.14), kind=kLoop, calls=%fused_computation.6 | loop fusion | bytes 1572876 | tf_op jit(solution)/shard_map/reshape | solution.py:301
  42.2 1.9 %collective-permute-start.3 = (f32[512,128]{1,0:T(8,128)}, f32[512,128]{1,0:T(8,128)}, u32[]{:S(2)}, u32[]{:S(2)}) collective-permute-start(f32[512,128]{1,0:T(8,128)} %get-tuple-element.55), channel_id=1, source_target_pairs={{0,1},{1,2},{2,3},{3,0},{4,5},{5,6},{6,7},{7,4},{8,9},{9,10},{10,1... | collective-permute-start | bytes 786440 | tf_op jit(solution)/shard_map/ppermute | solution.py:274
  44.2 27.2 %collective-permute-start.4 = (f32[512,128]{1,0:T(8,128)}, f32[512,128]{1,0:T(8,128)}, u32[]{:S(2)}, u32[]{:S(2)}) collective-permute-start(f32[512,128]{1,0:T(8,128)} %get-tuple-element.54), channel_id=1, source_target_pairs={{0,2},{1,3},{2,0},{3,1},{4,6},{5,7},{6,4},{7,5},{8,10},{9,11},{10,... | collective-permute-start | bytes 786440 | tf_op jit(solution)/shard_map/ppermute | solution.py:274
  72.1 4.1 %gram.4 = (bf16[4096,512]{1,0:T(8,128)(2,1)}, bf16[4096,512]{1,0:T(8,128)(2,1)}, f32[5,256,256]{2,1,0:T(8,128)}) custom-call(s32[2]{0:T(128)} %pad_add_fusion.place, f32[4,4096,128]{2,1,0:T(8,128)} %bitcast.40, f32[512,128]{1,0:T(8,128)} %copy-done.9, f32[512,128]{1,0:T(8,128)} %copy-done.10, f32[512,128]{1,0:T(8,128)} %copy-done.11, f32[1,512]{1,0:T(1,128)} %bitcast.47), custom_call_target="tpu_custom_call" | custom-call | flops 469762048 | bytes 2097152 | tf_op jit(solution)/shard_map/gram/pallas_call | solution.py:112
  76.2 4.0 %collective-permute-start.5 = (f32[512,128]{1,0:T(8,128)S(1)}, f32[512,128]{1,0:T(8,128)S(1)}, u32[]{:S(2)}, u32[]{:S(2)}) collective-permute-start(f32[512,128]{1,0:T(8,128)S(1)} %copy-done.8), channel_id=1, source_target_pairs={{0,3},{1,0},{2,1},{3,2},{4,7},{5,4},{6,5},{7,6},{8,11},{9,8},{10,9... | collective-permute-start | bytes 786440 | tf_op jit(solution)/shard_map/ppermute | solution.py:274
  80.2 4.4 %gram.5 = (bf16[4096,512]{1,0:T(8,128)(2,1)}, bf16[4096,512]{1,0:T(8,128)(2,1)}, f32[5,256,256]{2,1,0:T(8,128)}) custom-call(s32[2]{0:T(128)} %pad_add_fusion.place, f32[4,4096,128]{2,1,0:T(8,128)} %bitcast.41, f32[520,128]{1,0:T(8,128)} %copy-done.4, f32[520,128]{1,0:T(8,128)} %copy-done.5, ...), custom_call_target="tpu_custom_call", output_to_operand_aliasing={{2}: (6, {}), {0}: (7, {}), {1}: (8, {})} | custom-call | flops 469762048 | bytes 2097152 | tf_op jit(solution)/shard_map/gram/pallas_call | solution.py:112
  84.6 2.5 %collective-permute-done.11.back = f32[2560,128]{1,0:T(8,128)S(1)} collective-permute-done((f32[2560,128]{1,0:T(8,128)}, f32[2560,128]{1,0:T(8,128)S(1)}, u32[]{:S(2)}, u32[]{:S(2)}) %collective-permute-start.11) | collective-permute-done | bytes 1310752 | tf_op jit(solution)/shard_map/ppermute | solution.py:274
  88.2 8.8 %gram.6 = (bf16[4096,512]{1,0:T(8,128)(2,1)}, bf16[4096,512]{1,0:T(8,128)(2,1)}, f32[5,256,256]{2,1,0:T(8,128)}) custom-call(s32[2]{0:T(128)} %pad_add_fusion.place, f32[4,4096,128]{2,1,0:T(8,128)} %bitcast.42, f32[2560,128]{1,0:T(8,128)} %collective-permute-done.9.near, ...), custom_call_target="tpu_custom_call", output_to_operand_aliasing={{2}: (6, {}), {0}: (7, {}), {1}: (8, {})} | custom-call | flops 2348810240 | bytes 10485760 | tf_op jit(solution)/shard_map/gram/pallas_call | solution.py:112
  98.1 4.6 %gram.7 = (bf16[4096,512]{1,0:T(8,128)(2,1)}, bf16[4096,512]{1,0:T(8,128)(2,1)}, f32[5,256,256]{2,1,0:T(8,128)}, f32[5,128,128]{2,1,0:T(8,128)}, f32[5,128,128]{2,1,0:T(8,128)}) custom-call(s32[2]{0:T(128)} %pad_add_fusion.place, f32[4,4096,128]{2,1,0:T(8,128)} %bitcast.43, ...), custom_call_target="tpu_custom_call", output_to_operand_aliasing={{2}: (6, {}), {0}: (7, {}), {1}: (8, {})} | custom-call | flops 469762048 | bytes 2097152 | tf_op jit(solution)/shard_map/gram/pallas_call | solution.py:112
  102.7 1.8 %collective-permute-done.12 = f32[5,128,128]{2,1,0:T(8,128)S(1)} collective-permute-done((f32[5,128,128]{2,1,0:T(8,128)}, f32[5,128,128]{2,1,0:T(8,128)S(1)}, u32[]{:S(2)}, u32[]{:S(2)}) %collective-permute-start.12) | collective-permute-done | bytes 327712 | tf_op jit(solution)/shard_map/ppermute | solution.py:278
  105.5 17.1 %all_to_all.15 = f32[16,40,128]{2,1,0:T(8,128)S(1)} all-to-all(f32[16,40,128]{2,1,0:T(8,128)S(1)} %bitcast.46), channel_id=1, replica_groups=mesh['x'=4,'z'=4,'core'=2,'y'=4] {'x','z'}, dimensions={0} | all-to-all | bytes 655360 | tf_op jit(solution)/shard_map/all_to_all | solution.py:284
  124.5 2.2 %collective-permute-start.14 = (f32[40,128]{1,0:T(8,128)S(1)}, f32[40,128]{1,0:T(8,128)S(1)}, u32[]{:S(2)}, u32[]{:S(2)}) collective-permute-start(f32[40,128]{1,0:T(8,128)S(1)} %reduce_sum.29), channel_id=1, source_target_pairs={{0,2},{1,3},{2,0},{3,1},{4,6},{5,7},{6,4},{7,5},{8,10},{9,11},{10,... | collective-permute-start | bytes 61448 | tf_op jit(solution)/shard_map/ppermute | solution.py:278
  127.5 2.3 %collective-permute-done.14 = f32[40,128]{1,0:T(8,128)S(1)} collective-permute-done((f32[40,128]{1,0:T(8,128)S(1)}, f32[40,128]{1,0:T(8,128)S(1)}, u32[]{:S(2)}, u32[]{:S(2)}) %collective-permute-start.14) | collective-permute-done | bytes 20512 | tf_op jit(solution)/shard_map/ppermute | solution.py:278
  129.8 1.9 %collective-permute-done.15 = f32[40,128]{1,0:T(8,128)S(1)} collective-permute-done((f32[40,128]{1,0:T(8,128)S(1)}, f32[40,128]{1,0:T(8,128)S(1)}, u32[]{:S(2)}, u32[]{:S(2)}) %collective-permute-start.15) | collective-permute-done | bytes 20512 | tf_op jit(solution)/shard_map/ppermute | solution.py:278
  131.7 12.3 %all_to_all.16 = f32[16,40,128]{2,1,0:T(8,128)S(1)} all-to-all(f32[16,40,128]{2,1,0:T(8,128)S(1)} %broadcast_in_dim.15), channel_id=1, replica_groups=mesh['x'=4,'z'=4,'core'=2,'y'=4] {'x','z'}, dimensions={0} | all-to-all | bytes 655360 | tf_op jit(solution)/shard_map/all_to_all | solution.py:288
  146.4 26.6 %whiten.1 = (f32[4096,512]{1,0:T(8,128)}, f32[1,128]{1,0:T(1,128)}) custom-call(s32[2]{0:T(128)} %pad_add_fusion.place, f32[5,128,128]{2,1,0:T(8,128)} %bitcast.45, f32[5,128,128]{2,1,0:T(8,128)} %copy-done.3, bf16[4096,512]{1,0:T(8,128)(2,1)} %get-tuple-element.46.high_hbm, bf16[4096,512]{1,0:T(8,128)(2,1)} %get-tuple-element.47.low_hbm), custom_call_target="tpu_custom_call" | custom-call | tf_op jit(solution)/shard_map/whiten/pallas_call | solution.py:249
  (62 shorter events, 19.1 us)
Async XLA Ops:
  2.1 12.9 %collective-permute-start.6 = (f32[512,128]{1,0:T(8,128)S(1)}, f32[512,128]{1,0:T(8,128)S(1)}, u32[]{:S(2)}, u32[]{:S(2)}) collective-permute-start(f32[512,128]{1,0:T(8,128)S(1)} %get-tuple-element.60), channel_id=1, source_target_pairs={{0,1},{1,2},{2,3},{3,0},{4,5},{5,6},{6,7},{7,4},{8,9},{9,10},{10,1... | collective-permute-start | bytes 786440 | tf_op jit(solution)/shard_map/ppermute | solution.py:274
  3.8 15.7 %collective-permute-start.7 = (f32[512,128]{1,0:T(8,128)S(1)}, f32[512,128]{1,0:T(8,128)S(1)}, u32[]{:S(2)}, u32[]{:S(2)}) collective-permute-start(f32[512,128]{1,0:T(8,128)S(1)} %get-tuple-element.59), channel_id=1, source_target_pairs={{0,2},{1,3},{2,0},{3,1},{4,6},{5,7},{6,4},{7,5},{8,10},{9,11},{10,... | collective-permute-start | bytes 786440 | tf_op jit(solution)/shard_map/ppermute | solution.py:274
  6.7 12.8 %collective-permute-start.8 = (f32[512,128]{1,0:T(8,128)S(1)}, f32[512,128]{1,0:T(8,128)S(1)}, u32[]{:S(2)}, u32[]{:S(2)}) collective-permute-start(f32[512,128]{1,0:T(8,128)S(1)} %get-tuple-element.58), channel_id=1, source_target_pairs={{0,3},{1,0},{2,1},{3,2},{4,7},{5,4},{6,5},{7,6},{8,11},{9,8},{10,9... | collective-permute-start | bytes 786440 | tf_op jit(solution)/shard_map/ppermute | solution.py:274
  13.5 15.0 %collective-permute-start = (f32[520,128]{1,0:T(8,128)S(1)}, f32[520,128]{1,0:T(8,128)S(1)}, u32[]{:S(2)}, u32[]{:S(2)}) collective-permute-start(f32[520,128]{1,0:T(8,128)S(1)} %get-tuple-element.64), channel_id=1, source_target_pairs={{0,1},{1,2},{2,3},{3,0},{4,5},{5,6},{6,7},{7,4},{8,9},{9,10},{10,1... | collective-permute-start | bytes 798728 | tf_op jit(solution)/shard_map/ppermute | solution.py:274
  14.2 16.8 %collective-permute-start.1 = (f32[520,128]{1,0:T(8,128)}, f32[520,128]{1,0:T(8,128)S(1)}, u32[]{:S(2)}, u32[]{:S(2)}) collective-permute-start(f32[520,128]{1,0:T(8,128)} %get-tuple-element.63), channel_id=1, source_target_pairs={{0,2},{1,3},{2,0},{3,1},{4,6},{5,7},{6,4},{7,5},{8,10},{9,11},{10,... | collective-permute-start | bytes 798728 | tf_op jit(solution)/shard_map/ppermute | solution.py:274
  15.0 11.6 %copy-start.9 = (f32[512,128]{1,0:T(8,128)}, f32[512,128]{1,0:T(8,128)S(1)}, u32[]{:S(2)}) copy-start(f32[512,128]{1,0:T(8,128)S(1)} %collective-permute-done.6.near) | copy-start | bytes 786436
  15.0 16.0 %collective-permute-start.2 = (f32[520,128]{1,0:T(8,128)}, f32[520,128]{1,0:T(8,128)S(1)}, u32[]{:S(2)}, u32[]{:S(2)}) collective-permute-start(f32[520,128]{1,0:T(8,128)} %get-tuple-element.62), channel_id=1, source_target_pairs={{0,3},{1,0},{2,1},{3,2},{4,7},{5,4},{6,5},{7,6},{8,11},{9,8},{10,9... | collective-permute-start | bytes 798728 | tf_op jit(solution)/shard_map/ppermute | solution.py:274
  19.5 7.1 %copy-start.10 = (f32[512,128]{1,0:T(8,128)}, f32[512,128]{1,0:T(8,128)S(1)}, u32[]{:S(2)}) copy-start(f32[512,128]{1,0:T(8,128)S(1)} %collective-permute-done.7.far) | copy-start | bytes 786436
  23.8 52.3 %collective-permute-start.10 = (f32[2560,128]{1,0:T(8,128)}, f32[2560,128]{1,0:T(8,128)S(1)}, u32[]{:S(2)}, u32[]{:S(2)}) collective-permute-start(f32[2560,128]{1,0:T(8,128)} %get-tuple-element.51), channel_id=1, source_target_pairs={{0,2},{1,3},{2,0},{3,1},{4,6},{5,7},{6,4},{7,5},{8,10},{9,11},{10,... | collective-permute-start | bytes 3932168 | tf_op jit(solution)/shard_map/ppermute | solution.py:274
  26.6 60.5 %collective-permute-start.11 = (f32[2560,128]{1,0:T(8,128)}, f32[2560,128]{1,0:T(8,128)S(1)}, u32[]{:S(2)}, u32[]{:S(2)}) collective-permute-start(f32[2560,128]{1,0:T(8,128)} %get-tuple-element.50), channel_id=1, source_target_pairs={{0,3},{1,0},{2,1},{3,2},{4,7},{5,4},{6,5},{7,6},{8,11},{9,8},{10,9... | collective-permute-start | bytes 3932168 | tf_op jit(solution)/shard_map/ppermute | solution.py:274
  28.6 47.6 %copy-start.4 = (f32[520,128]{1,0:T(8,128)}, f32[520,128]{1,0:T(8,128)S(1)}, u32[]{:S(2)}) copy-start(f32[520,128]{1,0:T(8,128)S(1)} %collective-permute-done.near) | copy-start | bytes 798724
  28.6 58.5 %collective-permute-start.9 = (f32[2560,128]{1,0:T(8,128)}, f32[2560,128]{1,0:T(8,128)}, u32[]{:S(2)}, u32[]{:S(2)}) collective-permute-start(f32[2560,128]{1,0:T(8,128)} %get-tuple-element.52), channel_id=1, source_target_pairs={{0,1},{1,2},{2,3},{3,0},{4,5},{5,6},{6,7},{7,4},{8,9},{9,10},{10,1... | collective-permute-start | bytes 3932168 | tf_op jit(solution)/shard_map/ppermute | solution.py:274
  31.0 45.1 %copy-start.5 = (f32[520,128]{1,0:T(8,128)}, f32[520,128]{1,0:T(8,128)S(1)}, u32[]{:S(2)}) copy-start(f32[520,128]{1,0:T(8,128)S(1)} %collective-permute-done.1.far) | copy-start | bytes 798724
  31.0 45.1 %copy-start.6 = (f32[520,128]{1,0:T(8,128)}, f32[520,128]{1,0:T(8,128)S(1)}, u32[]{:S(2)}) copy-start(f32[520,128]{1,0:T(8,128)S(1)} %collective-permute-done.2.back) | copy-start | bytes 798724
  32.0 39.4 %all-to-all-start = ((f32[32,1,512]{2,1,0:T(1,128)}), f32[32,1,512]{2,1,0:T(1,128)S(1)}, u32[]{:S(2)}, u32[]{:S(2)}) async-start(f32[32,1,512]{2,1,0:T(1,128)} %broadcast_in_dim.14), calls=%async_computation | async-start | bytes 131072 | tf_op jit(solution)/shard_map/all_to_all | solution.py:320
  42.2 54.8 %collective-permute-start.3 = (f32[512,128]{1,0:T(8,128)}, f32[512,128]{1,0:T(8,128)}, u32[]{:S(2)}, u32[]{:S(2)}) collective-permute-start(f32[512,128]{1,0:T(8,128)} %get-tuple-element.55), channel_id=1, source_target_pairs={{0,1},{1,2},{2,3},{3,0},{4,5},{5,6},{6,7},{7,4},{8,9},{9,10},{10,1... | collective-permute-start | bytes 786440 | tf_op jit(solution)/shard_map/ppermute | solution.py:274
  44.2 53.2 %collective-permute-start.4 = (f32[512,128]{1,0:T(8,128)}, f32[512,128]{1,0:T(8,128)}, u32[]{:S(2)}, u32[]{:S(2)}) collective-permute-start(f32[512,128]{1,0:T(8,128)} %get-tuple-element.54), channel_id=1, source_target_pairs={{0,2},{1,3},{2,0},{3,1},{4,6},{5,7},{6,4},{7,5},{8,10},{9,11},{10,... | collective-permute-start | bytes 786440 | tf_op jit(solution)/shard_map/ppermute | solution.py:274
  76.2 8.5 %copy-start = (f32[2560,128]{1,0:T(8,128)}, f32[2560,128]{1,0:T(8,128)S(1)}, u32[]{:S(2)}) copy-start(f32[2560,128]{1,0:T(8,128)S(1)} %collective-permute-done.10.far) | copy-start | bytes 3932164
  76.2 21.2 %collective-permute-start.5 = (f32[512,128]{1,0:T(8,128)S(1)}, f32[512,128]{1,0:T(8,128)S(1)}, u32[]{:S(2)}, u32[]{:S(2)}) collective-permute-start(f32[512,128]{1,0:T(8,128)S(1)} %copy-done.8), channel_id=1, source_target_pairs={{0,3},{1,0},{2,1},{3,2},{4,7},{5,4},{6,5},{7,6},{8,11},{9,8},{10,9... | collective-permute-start | bytes 786440 | tf_op jit(solution)/shard_map/ppermute | solution.py:274
  102.7 1.8 %collective-permute-start.12 = (f32[5,128,128]{2,1,0:T(8,128)}, f32[5,128,128]{2,1,0:T(8,128)S(1)}, u32[]{:S(2)}, u32[]{:S(2)}) collective-permute-start(f32[5,128,128]{2,1,0:T(8,128)} %get-tuple-element.45), channel_id=1, source_target_pairs={{0,4},{4,0},{1,5},{5,1},{2,6},{6,2},{3,7},{7,3},{8,12},{12,8},{9,1... | collective-permute-start | bytes 983048 | tf_op jit(solution)/shard_map/ppermute | solution.py:278
  122.7 4.8 %collective-permute-start.13 = (f32[40,128]{1,0:T(8,128)S(1)}, f32[40,128]{1,0:T(8,128)S(1)}, u32[]{:S(2)}, u32[]{:S(2)}) collective-permute-start(f32[40,128]{1,0:T(8,128)S(1)} %reduce_sum.29), channel_id=1, source_target_pairs={{0,1},{1,0},{2,3},{3,2},{4,5},{5,4},{6,7},{7,6},{8,9},{9,8},{10,11... | collective-permute-start | bytes 61448 | tf_op jit(solution)/shard_map/ppermute | solution.py:278
  124.5 5.3 %collective-permute-start.14 = (f32[40,128]{1,0:T(8,128)S(1)}, f32[40,128]{1,0:T(8,128)S(1)}, u32[]{:S(2)}, u32[]{:S(2)}) collective-permute-start(f32[40,128]{1,0:T(8,128)S(1)} %reduce_sum.29), channel_id=1, source_target_pairs={{0,2},{1,3},{2,0},{3,1},{4,6},{5,7},{6,4},{7,5},{8,10},{9,11},{10,... | collective-permute-start | bytes 61448 | tf_op jit(solution)/shard_map/ppermute | solution.py:278
  126.7 5.0 %collective-permute-start.15 = (f32[40,128]{1,0:T(8,128)S(1)}, f32[40,128]{1,0:T(8,128)S(1)}, u32[]{:S(2)}, u32[]{:S(2)}) collective-permute-start(f32[40,128]{1,0:T(8,128)S(1)} %reduce_sum.29), channel_id=1, source_target_pairs={{0,3},{1,2},{2,1},{3,0},{4,7},{5,6},{6,5},{7,4},{8,11},{9,10},{10,... | collective-permute-start | bytes 61448 | tf_op jit(solution)/shard_map/ppermute | solution.py:278
  144.0 1.6 collective-permute-start.16
  (6 other events, 15.3 us)
